TPU v7x, 512 devices: a whole 4x8x8 slice. The times are simulated.
512 devices in a mesh: space: 64 (over z, x, core), years: 8 (over y).
Axes of the slice: x: 4, y: 8, z: 8, core: 2. Of those that a mesh axis runs over, the one named last changes fastest.
Arguments:
- maxima: float32 [32, 8, 1024, 640], P('years', None, 'space'), as said below
- fields: float32 [3, 1024, 640], P(None, 'space'), may hold values from -0.7 to 2, as said below
- kappa_sq: float32 [3, 1024, 640], P(None, 'space'), may hold values from 0.05 to 0.4
- anisotropy: float32 [3, 2], replicated, may hold values from 0.05 to 0.15
- precision: float32 [3], replicated, may hold values from 4 to 40
- ocean_mask: int32 [1024, 640], P('space'), may hold values from 0 to 1, as said below
- year_valid: int32 [32], P('years'), may hold values from 0 to 1, as said below
- counts: int32 [1024, 640], P('space'), may hold values from 1 to 8
Outputs:
- gradient: float32 [3, 1024, 640], P(None, 'space')
Inputs may be any that keep to these rules, and one draw needn't show every extreme that they name: `maxima`: for each year and cell the values fall strictly with the order. fields[0] lies in 1 to 2, fields[1] in -0.7 to 0, fields[2] in 0.1 to 0.3. `ocean_mask`: every cell of latitude 640 // 2 is ocean. `year_valid`: the last year is valid, and at least one other year is padded.
All inputs are finite; a program needn't handle non-finite values.
Results may differ from a plain program's by a relative error of at most 0.0003.
Values sent between devices are 32-bit elements; how exact they have to be, the bound alone decides.
No kernel may reach another device: no remote copies, remote signals or barrier semaphores. Data moves between devices by JAX's collectives and lax.ppermute only.
A program may use at most 64 MiB of HBM per device.

v0:
```python
import jax
import jax.numpy as jnp
from jax import lax
from jax.sharding import PartitionSpec as P

SWEEPS = 8


def extended(block, sides, width):
    for axis, dim in sides:
        count = lax.axis_size(axis)
        forward = [(i, i + 1) for i in range(count - 1)]
        forward.append((count - 1, 0))
        backward = [(target, source) for source, target in forward]
        low = lax.ppermute(
            lax.slice_in_dim(block, block.shape[dim] - width, None, axis=dim), axis, forward
        )
        high = lax.ppermute(lax.slice_in_dim(block, 0, width, axis=dim), axis, backward)
        block = jnp.concatenate([low, block, high], axis=dim)
    return block


def local_loss(fields, maxima, year_valid, ocean_mask, counts):
    location = fields[0]
    log_scale = fields[1]
    tail_shape = fields[2]
    reduced = 1.0 + tail_shape * (maxima - location) / jnp.exp(log_scale)
    log_reduced = jnp.log(reduced)
    order_index = jnp.arange(maxima.shape[1], dtype=jnp.int32).reshape(1, -1, 1, 1)
    order_used = order_index < counts[None, None]
    order_last = order_index == counts[None, None] - 1
    tail_term = jnp.exp(-jnp.sum(jnp.where(order_last, log_reduced, 0.0), axis=1) / tail_shape)
    order_terms = jnp.sum(
        jnp.where(order_used, log_scale + (1.0 + 1.0 / tail_shape) * log_reduced, 0.0), axis=1
    )
    weight = (year_valid[:, None, None] * ocean_mask[None]).astype(jnp.float32)
    return jnp.sum(weight * (tail_term + order_terms))


def sweep_cells(widened, kappa_rows, inside, zonal_weight, meridional_weight):
    centre_value = widened[:, 1:-1, 1:-1]
    east_west = widened[:, 2:, 1:-1] + widened[:, :-2, 1:-1]
    north_south = widened[:, 1:-1, 2:] + widened[:, 1:-1, :-2]
    result = (
        (kappa_rows + 2.0 * zonal_weight + 2.0 * meridional_weight) * centre_value
        - zonal_weight * east_west
        - meridional_weight * north_south
    )
    return result * inside


def prior_part(fields, kappa_sq, anisotropy, precision, first_row, row_count):
    margin = SWEEPS
    row_total = fields.shape[2]
    extent = row_count + 2 * margin
    padded_fields = jnp.pad(fields, ((0, 0), (0, 0), (margin, margin)))
    padded_kappa = jnp.pad(kappa_sq, ((0, 0), (0, 0), (margin, margin)))
    current = padded_fields
    global_row = first_row - margin + jnp.arange(extent, dtype=jnp.int32)
    inside = ((global_row >= 0) & (global_row < row_total)).astype(jnp.float32)
    zonal_weight = anisotropy[:, 0].reshape(3, 1, 1)
    meridional_weight = anisotropy[:, 1].reshape(3, 1, 1)
    for sweep_index in range(SWEEPS):
        widened = extended(current, (("space", 1),), 1)
        current = sweep_cells(
            widened,
            padded_kappa[:, :, sweep_index + 1 : extent - 1 - sweep_index],
            inside[sweep_index + 1 : extent - 1 - sweep_index],
            zonal_weight,
            meridional_weight,
        )
    return precision.reshape(3, 1, 1) * current


def local(maxima, fields, kappa_sq, anisotropy, precision, ocean_mask, year_valid, counts):
    cell_local = jnp.sum(ocean_mask * counts).astype(jnp.float32)
    year_local = jnp.sum(year_valid).astype(jnp.float32)
    observations = lax.psum(cell_local * year_local, ("space", "years"))
    likelihood = jax.grad(local_loss)(fields, maxima, year_valid, ocean_mask, counts)
    row_total = fields.shape[2]
    grid_cells = fields.shape[1] * lax.axis_size("space") * row_total
    cell_scale = jnp.float32(grid_cells) / observations
    summed = lax.psum(likelihood, "years")
    return summed * cell_scale + prior_part(fields, kappa_sq, anisotropy, precision, 0, row_total)


def solution(mesh):
    return jax.shard_map(
        local,
        mesh=mesh,
        in_specs=(
            P("years", None, "space", None),
            P(None, "space", None),
            P(None, "space", None),
            P(),
            P(),
            P("space", None),
            P("years"),
            P("space", None),
        ),
        out_specs=P(None, "space", None),
        check_vma=False,
    )
```

profile of v0, /device:TPU:1, one launch (start us, length us, event | category | flops | bytes accessed | tf_op | source)
XLA Modules:
  0.0 213.6 jit_solution(16266498628970926801)
XLA Ops:
  7.5 8.8 %collective-permute-start = (f32[3,1,656]{2,1,0:T(1,128)S(1)}, f32[3,1,656]{2,1,0:T(1,128)S(1)}, u32[]{:S(2)}, u32[]{:S(2)}) collective-permute-start(f32[3,1,656]{2,1,0:T(1,128)S(1)} %get-tuple-element.34), channel_id=1, source_target_pairs={{8,0},{16,8},{24,16},{32,24},{40,32},{48,40},{56,48},{64,56},{72,6... | collective-permute-start | bytes 23624 | tf_op jit(solution)/shard_map/ppermute | solution.py:18
  16.3 1.9 collective-permute-start.1
  20.6 1.4 multiply_reduce_fusion.4
  23.0 1.7 select_reduce_fusion.1
  25.4 7.3 %collective-permute-start.2 = (f32[3,1,654]{2,1,0:T(1,128)S(1)}, f32[3,1,654]{2,1,0:T(1,128)S(1)}, u32[]{:S(2)}, u32[]{:S(2)}) collective-permute-start(f32[3,1,654]{2,1,0:T(1,128)S(1)} %get-tuple-element.24), channel_id=1, source_target_pairs={{8,0},{16,8},{24,16},{32,24},{40,32},{48,40},{56,48},{64,56},{72,6... | collective-permute-start | bytes 23552 | tf_op jit(solution)/shard_map/ppermute | solution.py:18
  32.8 1.9 collective-permute-start.3
  34.8 5.6 %collective-permute-done.3 = f32[3,1,654]{2,1,0:T(1,128)S(1)} collective-permute-done((f32[3,1,654]{2,1,0:T(1,128)S(1)}, f32[3,1,654]{2,1,0:T(1,128)S(1)}, u32[]{:S(2)}, u32[]{:S(2)}) %collective-permute-start.3) | collective-permute-done | bytes 7880 | tf_op jit(solution)/shard_map/ppermute | solution.py:15
  40.8 7.6 %collective-permute-start.4 = (f32[3,1,652]{2,1,0:T(1,128)S(1)}, f32[3,1,652]{2,1,0:T(1,128)S(1)}, u32[]{:S(2)}, u32[]{:S(2)}) collective-permute-start(f32[3,1,652]{2,1,0:T(1,128)S(1)} %get-tuple-element.22), channel_id=1, source_target_pairs={{8,0},{16,8},{24,16},{32,24},{40,32},{48,40},{56,48},{64,56},{72,6... | collective-permute-start | bytes 23480 | tf_op jit(solution)/shard_map/ppermute | solution.py:18
  48.4 1.9 collective-permute-start.5
  51.8 7.2 %collective-permute-start.6 = (f32[3,1,650]{2,1,0:T(1,128)S(1)}, f32[3,1,650]{2,1,0:T(1,128)S(1)}, u32[]{:S(2)}, u32[]{:S(2)}) collective-permute-start(f32[3,1,650]{2,1,0:T(1,128)S(1)} %get-tuple-element.20), channel_id=1, source_target_pairs={{8,0},{16,8},{24,16},{32,24},{40,32},{48,40},{56,48},{64,56},{72,6... | collective-permute-start | bytes 23408 | tf_op jit(solution)/shard_map/ppermute | solution.py:18
  59.0 1.9 collective-permute-start.7
  60.9 1.1 multiply_reduce_fusion.2
  62.4 7.1 %collective-permute-start.8 = (f32[3,1,648]{2,1,0:T(1,128)S(1)}, f32[3,1,648]{2,1,0:T(1,128)S(1)}, u32[]{:S(2)}, u32[]{:S(2)}) collective-permute-start(f32[3,1,648]{2,1,0:T(1,128)S(1)} %get-tuple-element.18), channel_id=1, source_target_pairs={{8,0},{16,8},{24,16},{32,24},{40,32},{48,40},{56,48},{64,56},{72,6... | collective-permute-start | bytes 23336 | tf_op jit(solution)/shard_map/ppermute | solution.py:18
  69.5 1.9 collective-permute-start.9
  71.6 1.0 collective-permute-done.9
  73.0 7.2 %collective-permute-start.10 = (f32[3,1,646]{2,1,0:T(1,128)S(1)}, f32[3,1,646]{2,1,0:T(1,128)S(1)}, u32[]{:S(2)}, u32[]{:S(2)}) collective-permute-start(f32[3,1,646]{2,1,0:T(1,128)S(1)} %get-tuple-element.16), channel_id=1, source_target_pairs={{8,0},{16,8},{24,16},{32,24},{40,32},{48,40},{56,48},{64,56},{72,6... | collective-permute-start | bytes 23264 | tf_op jit(solution)/shard_map/ppermute | solution.py:18
  80.1 1.9 collective-permute-start.11
  82.1 1.1 collective-permute-done.11
  83.5 7.2 %collective-permute-start.12 = (f32[3,1,644]{2,1,0:T(1,128)S(1)}, f32[3,1,644]{2,1,0:T(1,128)S(1)}, u32[]{:S(2)}, u32[]{:S(2)}) collective-permute-start(f32[3,1,644]{2,1,0:T(1,128)S(1)} %get-tuple-element.14), channel_id=1, source_target_pairs={{8,0},{16,8},{24,16},{32,24},{40,32},{48,40},{56,48},{64,56},{72,6... | collective-permute-start | bytes 23192 | tf_op jit(solution)/shard_map/ppermute | solution.py:18
  90.7 1.9 collective-permute-start.13
  94.1 7.2 %collective-permute-start.14 = (f32[3,1,642]{2,1,0:T(1,128)S(1)}, f32[3,1,642]{2,1,0:T(1,128)S(1)}, u32[]{:S(2)}, u32[]{:S(2)}) collective-permute-start(f32[3,1,642]{2,1,0:T(1,128)S(1)} %get-tuple-element.12), channel_id=1, source_target_pairs={{8,0},{16,8},{24,16},{32,24},{40,32},{48,40},{56,48},{64,56},{72,6... | collective-permute-start | bytes 23120 | tf_op jit(solution)/shard_map/ppermute | solution.py:18
  101.3 1.9 collective-permute-start.15
  104.9 99.4 %psum.15 = f32[]{:T(128)} all-reduce(f32[]{:T(128)S(6)} %mul.381), channel_id=1, replica_groups=mesh['space'=64,'years'=8] {'space','years'}, use_global_device_ids=true, to_apply=%region_10.11 | all-reduce | flops 1 | bytes 8 | tf_op jit(solution)/shard_map/psum | solution.py:78
  205.0 1.8 fusion.68
  (67 shorter events, 10.2 us)
Async XLA Ops:
  6.5 18.2 %copy-start.3 = (s32[16,640]{1,0:T(8,128)S(1)}, s32[16,640]{1,0:T(8,128)}, u32[]{:S(2)}) copy-start(s32[16,640]{1,0:T(8,128)} %param.13) | copy-start | bytes 122884
  6.5 18.2 %copy-start.5 = (s32[4]{0:T(128)S(1)}, s32[4]{0:T(128)}, u32[]{:S(2)}) copy-start(s32[4]{0:T(128)} %param.14) | copy-start | bytes 52
  6.5 198.4 %all-reduce.7.cloned.1.call-start = ((), (), s32[]{:S(2)}) async-start(), calls=%async_computation | async-start | bytes 245760 | tf_op jit(solution)/shard_map/psum | solution.py:83
  7.5 17.5 %collective-permute-start = (f32[3,1,656]{2,1,0:T(1,128)S(1)}, f32[3,1,656]{2,1,0:T(1,128)S(1)}, u32[]{:S(2)}, u32[]{:S(2)}) collective-permute-start(f32[3,1,656]{2,1,0:T(1,128)S(1)} %get-tuple-element.34), channel_id=1, source_target_pairs={{8,0},{16,8},{24,16},{32,24},{40,32},{48,40},{56,48},{64,56},{72,6... | collective-permute-start | bytes 23624 | tf_op jit(solution)/shard_map/ppermute | solution.py:18
  16.3 8.8 %collective-permute-start.1 = (f32[3,1,656]{2,1,0:T(1,128)S(1)}, f32[3,1,656]{2,1,0:T(1,128)S(1)}, u32[]{:S(2)}, u32[]{:S(2)}) collective-permute-start(f32[3,1,656]{2,1,0:T(1,128)S(1)} %get-tuple-element.35), channel_id=1, source_target_pairs={{0,8},{8,16},{16,24},{24,32},{32,40},{40,48},{48,56},{56,64},{64,7... | collective-permute-start | bytes 23624 | tf_op jit(solution)/shard_map/ppermute | solution.py:15
  20.6 4.4 %copy-start.2 = (f32[3,16,640]{2,1,0:T(8,128)S(1)}, f32[3,16,640]{2,1,0:T(8,128)}, u32[]{:S(2)}) copy-start(f32[3,16,640]{2,1,0:T(8,128)} %param.9) | copy-start | bytes 368644
  22.1 3.0 %copy-start = (f32[3,16,640]{2,1,0:T(8,128)S(1)}, f32[3,16,640]{2,1,0:T(8,128)}, u32[]{:S(2)}) copy-start(f32[3,16,640]{2,1,0:T(8,128)} %param.10) | copy-start | bytes 368644
  24.7 25.6 %copy-start.4 = (s32[16,640]{1,0:T(8,128)S(1)}, s32[16,640]{1,0:T(8,128)}, u32[]{:S(2)}) copy-start(s32[16,640]{1,0:T(8,128)} %param.15) | copy-start | bytes 122884
  25.4 35.5 %copy-start.1 = (f32[4,8,16,640]{3,2,1,0:T(8,128)S(1)}, f32[4,8,16,640]{3,2,1,0:T(8,128)}, u32[]{:S(2)}) copy-start(f32[4,8,16,640]{3,2,1,0:T(8,128)} %param.8) | copy-start | bytes 3932164
  25.4 9.4 %collective-permute-start.2 = (f32[3,1,654]{2,1,0:T(1,128)S(1)}, f32[3,1,654]{2,1,0:T(1,128)S(1)}, u32[]{:S(2)}, u32[]{:S(2)}) collective-permute-start(f32[3,1,654]{2,1,0:T(1,128)S(1)} %get-tuple-element.24), channel_id=1, source_target_pairs={{8,0},{16,8},{24,16},{32,24},{40,32},{48,40},{56,48},{64,56},{72,6... | collective-permute-start | bytes 23552 | tf_op jit(solution)/shard_map/ppermute | solution.py:18
  32.8 7.6 %collective-permute-start.3 = (f32[3,1,654]{2,1,0:T(1,128)S(1)}, f32[3,1,654]{2,1,0:T(1,128)S(1)}, u32[]{:S(2)}, u32[]{:S(2)}) collective-permute-start(f32[3,1,654]{2,1,0:T(1,128)S(1)} %get-tuple-element.25), channel_id=1, source_target_pairs={{0,8},{8,16},{16,24},{24,32},{32,40},{40,48},{48,56},{56,64},{64,7... | collective-permute-start | bytes 23552 | tf_op jit(solution)/shard_map/ppermute | solution.py:15
  40.8 9.7 %collective-permute-start.4 = (f32[3,1,652]{2,1,0:T(1,128)S(1)}, f32[3,1,652]{2,1,0:T(1,128)S(1)}, u32[]{:S(2)}, u32[]{:S(2)}) collective-permute-start(f32[3,1,652]{2,1,0:T(1,128)S(1)} %get-tuple-element.22), channel_id=1, source_target_pairs={{8,0},{16,8},{24,16},{32,24},{40,32},{48,40},{56,48},{64,56},{72,6... | collective-permute-start | bytes 23480 | tf_op jit(solution)/shard_map/ppermute | solution.py:18
  48.4 3.1 %collective-permute-start.5 = (f32[3,1,652]{2,1,0:T(1,128)S(1)}, f32[3,1,652]{2,1,0:T(1,128)S(1)}, u32[]{:S(2)}, u32[]{:S(2)}) collective-permute-start(f32[3,1,652]{2,1,0:T(1,128)S(1)} %get-tuple-element.23), channel_id=1, source_target_pairs={{0,8},{8,16},{16,24},{24,32},{32,40},{40,48},{48,56},{56,64},{64,7... | collective-permute-start | bytes 23480 | tf_op jit(solution)/shard_map/ppermute | solution.py:15
  51.8 10.3 %collective-permute-start.6 = (f32[3,1,650]{2,1,0:T(1,128)S(1)}, f32[3,1,650]{2,1,0:T(1,128)S(1)}, u32[]{:S(2)}, u32[]{:S(2)}) collective-permute-start(f32[3,1,650]{2,1,0:T(1,128)S(1)} %get-tuple-element.20), channel_id=1, source_target_pairs={{8,0},{16,8},{24,16},{32,24},{40,32},{48,40},{56,48},{64,56},{72,6... | collective-permute-start | bytes 23408 | tf_op jit(solution)/shard_map/ppermute | solution.py:18
  59.0 3.1 %collective-permute-start.7 = (f32[3,1,650]{2,1,0:T(1,128)S(1)}, f32[3,1,650]{2,1,0:T(1,128)S(1)}, u32[]{:S(2)}, u32[]{:S(2)}) collective-permute-start(f32[3,1,650]{2,1,0:T(1,128)S(1)} %get-tuple-element.21), channel_id=1, source_target_pairs={{0,8},{8,16},{16,24},{24,32},{32,40},{40,48},{48,56},{56,64},{64,7... | collective-permute-start | bytes 23408 | tf_op jit(solution)/shard_map/ppermute | solution.py:15
  62.4 9.1 %collective-permute-start.8 = (f32[3,1,648]{2,1,0:T(1,128)S(1)}, f32[3,1,648]{2,1,0:T(1,128)S(1)}, u32[]{:S(2)}, u32[]{:S(2)}) collective-permute-start(f32[3,1,648]{2,1,0:T(1,128)S(1)} %get-tuple-element.18), channel_id=1, source_target_pairs={{8,0},{16,8},{24,16},{32,24},{40,32},{48,40},{56,48},{64,56},{72,6... | collective-permute-start | bytes 23336 | tf_op jit(solution)/shard_map/ppermute | solution.py:18
  69.5 3.1 %collective-permute-start.9 = (f32[3,1,648]{2,1,0:T(1,128)S(1)}, f32[3,1,648]{2,1,0:T(1,128)S(1)}, u32[]{:S(2)}, u32[]{:S(2)}) collective-permute-start(f32[3,1,648]{2,1,0:T(1,128)S(1)} %get-tuple-element.19), channel_id=1, source_target_pairs={{0,8},{8,16},{16,24},{24,32},{32,40},{40,48},{48,56},{56,64},{64,7... | collective-permute-start | bytes 23336 | tf_op jit(solution)/shard_map/ppermute | solution.py:15
  72.9 132.0 %copy-start.6 = (f32[3]{0:T(128)S(1)}, f32[3]{0:T(128)}, u32[]{:S(2)}) copy-start(f32[3]{0:T(128)} %param.12) | copy-start | bytes 40
  73.0 9.2 %collective-permute-start.10 = (f32[3,1,646]{2,1,0:T(1,128)S(1)}, f32[3,1,646]{2,1,0:T(1,128)S(1)}, u32[]{:S(2)}, u32[]{:S(2)}) collective-permute-start(f32[3,1,646]{2,1,0:T(1,128)S(1)} %get-tuple-element.16), channel_id=1, source_target_pairs={{8,0},{16,8},{24,16},{32,24},{40,32},{48,40},{56,48},{64,56},{72,6... | collective-permute-start | bytes 23264 | tf_op jit(solution)/shard_map/ppermute | solution.py:18
  80.1 3.1 %collective-permute-start.11 = (f32[3,1,646]{2,1,0:T(1,128)S(1)}, f32[3,1,646]{2,1,0:T(1,128)S(1)}, u32[]{:S(2)}, u32[]{:S(2)}) collective-permute-start(f32[3,1,646]{2,1,0:T(1,128)S(1)} %get-tuple-element.17), channel_id=1, source_target_pairs={{0,8},{8,16},{16,24},{24,32},{32,40},{40,48},{48,56},{56,64},{64,7... | collective-permute-start | bytes 23264 | tf_op jit(solution)/shard_map/ppermute | solution.py:15
  83.5 9.8 %collective-permute-start.12 = (f32[3,1,644]{2,1,0:T(1,128)S(1)}, f32[3,1,644]{2,1,0:T(1,128)S(1)}, u32[]{:S(2)}, u32[]{:S(2)}) collective-permute-start(f32[3,1,644]{2,1,0:T(1,128)S(1)} %get-tuple-element.14), channel_id=1, source_target_pairs={{8,0},{16,8},{24,16},{32,24},{40,32},{48,40},{56,48},{64,56},{72,6... | collective-permute-start | bytes 23192 | tf_op jit(solution)/shard_map/ppermute | solution.py:18
  90.7 3.1 %collective-permute-start.13 = (f32[3,1,644]{2,1,0:T(1,128)S(1)}, f32[3,1,644]{2,1,0:T(1,128)S(1)}, u32[]{:S(2)}, u32[]{:S(2)}) collective-permute-start(f32[3,1,644]{2,1,0:T(1,128)S(1)} %get-tuple-element.15), channel_id=1, source_target_pairs={{0,8},{8,16},{16,24},{24,32},{32,40},{40,48},{48,56},{56,64},{64,7... | collective-permute-start | bytes 23192 | tf_op jit(solution)/shard_map/ppermute | solution.py:15
  94.1 110.8 %collective-permute-start.14 = (f32[3,1,642]{2,1,0:T(1,128)S(1)}, f32[3,1,642]{2,1,0:T(1,128)S(1)}, u32[]{:S(2)}, u32[]{:S(2)}) collective-permute-start(f32[3,1,642]{2,1,0:T(1,128)S(1)} %get-tuple-element.12), channel_id=1, source_target_pairs={{8,0},{16,8},{24,16},{32,24},{40,32},{48,40},{56,48},{64,56},{72,6... | collective-permute-start | bytes 23120 | tf_op jit(solution)/shard_map/ppermute | solution.py:18
  101.3 103.7 %collective-permute-start.15 = (f32[3,1,642]{2,1,0:T(1,128)S(1)}, f32[3,1,642]{2,1,0:T(1,128)S(1)}, u32[]{:S(2)}, u32[]{:S(2)}) collective-permute-start(f32[3,1,642]{2,1,0:T(1,128)S(1)} %get-tuple-element.13), channel_id=1, source_target_pairs={{0,8},{8,16},{16,24},{24,32},{32,40},{40,48},{48,56},{56,64},{64,7... | collective-permute-start | bytes 23120 | tf_op jit(solution)/shard_map/ppermute | solution.py:15
Sparse Core Ops, SparseCore 0:
  93.4 69.7 all-reduce.6
where the time goes:
time: 214 us
  blocking collectives  99.4 us (46%)
  starting transfers between devices  74.8 us (35%)
  between operations  15.5 us (7%)
  other arithmetic  12.3 us (6%)
  waiting for transfers between devices  9.11 us (4%)
  local copies, waits for them, and re-layouts  2.54 us (1%)
    psum x1, blocking collectives, local(): observations = lax.psum(cell_local * year_local, ('space', 'years'))  99.4 us
    ppermute x8, starting transfers between devices, extended(): lax.ppermute(lax.slice_in_dim(block, 0, width, axis=dim), axis, backward)  59.5 us
    ppermute x8, starting transfers between devices, extended(): lax.ppermute(lax.slice_in_dim(block, block.shape[dim] - width, None, axis...  15.4 us
    ppermute x8, waiting for transfers between devices, extended(): lax.ppermute(lax.slice_in_dim(block, block.shape[dim] - width, None, axis...  9.05 us
  transfers between devices with their start and end apart: 17, of which 5 were waited for; matrix products, arithmetic and copies ran while one was open for 5% of the time, Pallas kernels for 0%

commit v1 on v0

v1 whole, which is shorter than its diff:
```python
import jax
import jax.numpy as jnp
from jax import lax
from jax.experimental import pallas as pl
from jax.experimental.pallas import tpu as pltpu
from jax.sharding import PartitionSpec as P

SWEEPS = 8
HALO = 8
LANES = 128
SUB = 8
VMEM = pl.BlockSpec(memory_space=pltpu.VMEM)
SMEM = pl.BlockSpec(memory_space=pltpu.SMEM)


def likelihood_kernel(
    valid_ref, maxima_ref, fields_ref, kappa_ref, mask_ref, counts_ref,
    tiles_ref, cells_ref, low_ref, high_ref,
):
    years, orders, rows, columns = maxima_ref.shape
    row_tiles, lane_tiles = rows // SUB, columns // LANES
    valid = [valid_ref[t].astype(jnp.float32) for t in range(years)]
    valid_sum = sum(valid[1:], valid[0])
    cells = jnp.zeros((SUB, LANES), jnp.float32)
    for r in range(row_tiles):
        for c in range(lane_tiles):
            at = (pl.ds(r * SUB, SUB), pl.ds(c * LANES, LANES))
            location = fields_ref[(0,) + at]
            log_scale = fields_ref[(1,) + at]
            shape = fields_ref[(2,) + at]
            count = counts_ref[at]
            mask = mask_ref[at].astype(jnp.float32)
            inv_scale = jnp.exp(-log_scale)
            inv_shape = 1.0 / shape
            slope = shape * inv_scale
            sum_inv = jnp.zeros((SUB, LANES), jnp.float32)
            sum_log = jnp.zeros((SUB, LANES), jnp.float32)
            tail_sum = jnp.zeros((SUB, LANES), jnp.float32)
            tail_inv = jnp.zeros((SUB, LANES), jnp.float32)
            tail_log = jnp.zeros((SUB, LANES), jnp.float32)
            for t in range(years):
                inv_t = None
                for k in range(orders):
                    reduced = 1.0 + slope * (maxima_ref[(t, k) + at] - location)
                    if k == 0:
                        used, last = reduced, reduced
                    else:
                        is_used = count > k
                        used = jnp.where(is_used, reduced, 1.0)
                        last = jnp.where(is_used, reduced, last)
                    inv = 1.0 - 1.0 / used
                    log = jnp.log(used)
                    if k == 0:
                        inv_t, log_t = inv, log
                    else:
                        inv_t, log_t = inv_t + inv, log_t + log
                last_log = jnp.log(last)
                tail = jnp.exp(-last_log * inv_shape) * valid[t]
                sum_inv = sum_inv + inv_t * valid[t]
                sum_log = sum_log + log_t * valid[t]
                tail_sum = tail_sum + tail
                tail_inv = tail_inv + tail / last
                tail_log = tail_log + tail * last_log
            used_total = valid_sum * count.astype(jnp.float32)
            one_more = 1.0 + inv_shape
            tail_diff = tail_sum - tail_inv
            grad = (
                (tail_inv - (1.0 + shape) * (used_total - sum_inv)) * inv_scale,
                used_total - one_more * sum_inv + tail_diff * inv_shape,
                (
                    (tail_log - sum_log - tail_diff) * inv_shape
                    + one_more * sum_inv
                ) * inv_shape,
            )
            for f in range(3):
                tiles_ref[(f * row_tiles + r) * lane_tiles + c] = grad[f] * mask
            cells = cells + mask * count.astype(jnp.float32)
    used_tiles = 3 * row_tiles * lane_tiles
    tiles_ref[used_tiles] = jnp.full((SUB, LANES), valid_sum, jnp.float32)
    for q in range(used_tiles + 1, tiles_ref.shape[0]):
        tiles_ref[q] = jnp.zeros((SUB, LANES), jnp.float32)
    cells_ref[...] = jnp.broadcast_to(
        jnp.sum(cells, axis=0, keepdims=True), cells_ref.shape
    )
    low_ref[0:3] = fields_ref[:, 0:HALO]
    low_ref[3:6] = kappa_ref[:, 0:HALO]
    high_ref[0:3] = fields_ref[:, rows - HALO : rows]
    high_ref[3:6] = kappa_ref[:, rows - HALO : rows]


def middle_kernel(parts_ref, out_ref):
    groups = parts_ref.shape[0]
    total = parts_ref[0]
    for g in range(1, groups):
        total = total + parts_ref[g]
    for g in range(groups):
        out_ref[g] = total


def prior_kernel(aniso_ref, precision_ref, fields_ref, kappa_ref, low_ref, high_ref, out_ref):
    rows, columns = fields_ref.shape[1:]
    extent = rows + 2 * HALO
    lane = lax.broadcasted_iota(jnp.int32, (extent, columns), 1)
    for f in range(3):
        zonal, meridional = aniso_ref[f, 0], aniso_ref[f, 1]
        values = jnp.concatenate([low_ref[f], fields_ref[f], high_ref[f]], axis=0)
        centre = jnp.concatenate([low_ref[3 + f], kappa_ref[f], high_ref[3 + f]], axis=0)
        centre = centre + (2.0 * zonal + 2.0 * meridional)
        for _ in range(SWEEPS):
            east_west = pltpu.roll(values, 1, 0) + pltpu.roll(values, extent - 1, 0)
            south = jnp.where(lane == 0, 0.0, pltpu.roll(values, 1, 1))
            north = jnp.where(lane == columns - 1, 0.0, pltpu.roll(values, columns - 1, 1))
            values = centre * values - zonal * east_west - meridional * (south + north)
        out_ref[f] = precision_ref[f] * values[HALO : HALO + rows]


def final_kernel(grid_cells, tiles_ref, cells_ref, prior_ref, out_ref):
    rows, columns = out_ref.shape[1:]
    row_tiles, lane_tiles = rows // SUB, columns // LANES
    cell_count = jnp.sum(
        jnp.sum(cells_ref[...], axis=0, keepdims=True), axis=1, keepdims=True
    )
    year_count = tiles_ref[3 * row_tiles * lane_tiles, 0:1, 0:1]
    scale = jnp.broadcast_to(grid_cells / (cell_count * year_count), (SUB, LANES))
    for f in range(3):
        for r in range(row_tiles):
            for c in range(lane_tiles):
                at = (f, pl.ds(r * SUB, SUB), pl.ds(c * LANES, LANES))
                tile = tiles_ref[(f * row_tiles + r) * lane_tiles + c]
                out_ref[at] = tile * scale + prior_ref[at]


def shifted(axis, step):
    count = lax.axis_size(axis)
    return [(i, (i + step) % count) for i in range(count)]


def local(maxima, fields, kappa_sq, anisotropy, precision, ocean_mask, year_valid, counts):
    f32 = jnp.float32
    rows, columns = fields.shape[1:]
    spaces, groups = lax.axis_size("space"), lax.axis_size("years")
    used_tiles = 3 * (rows // SUB) * (columns // LANES) + 1
    tile_count = -(-used_tiles // groups) * groups
    tiles_shape = jax.ShapeDtypeStruct((tile_count, SUB, LANES), f32)
    halo_shape = jax.ShapeDtypeStruct((6, HALO, columns), f32)
    tiles, cells, low, high = pl.pallas_call(
        likelihood_kernel,
        out_shape=(tiles_shape, jax.ShapeDtypeStruct((spaces, LANES), f32), halo_shape, halo_shape),
        in_specs=[SMEM] + [VMEM] * 5,
        out_specs=(VMEM,) * 4,
        cost_estimate=pl.CostEstimate(
            flops=20 * maxima.size, bytes_accessed=4 * maxima.size, transcendentals=2 * maxima.size
        ),
        name="likelihood",
    )(year_valid, maxima, fields, kappa_sq, ocean_mask, counts)

    parts = lax.all_to_all(tiles, "years", 0, 0, tiled=True)
    from_low = lax.ppermute(high, "space", shifted("space", 1))
    from_high = lax.ppermute(low, "space", shifted("space", -1))
    cell_parts = lax.all_to_all(cells, "space", 0, 0, tiled=True)

    spread = pl.pallas_call(
        middle_kernel,
        out_shape=jax.ShapeDtypeStruct((groups, tile_count // groups, SUB, LANES), f32),
        in_specs=[VMEM],
        out_specs=VMEM,
        cost_estimate=pl.CostEstimate(flops=tiles.size, bytes_accessed=8 * tiles.size, transcendentals=0),
        name="middle",
    )(parts.reshape(groups, tile_count // groups, SUB, LANES))
    summed = lax.all_to_all(
        spread.reshape(tile_count, SUB, LANES), "years", 0, 0, tiled=True
    )

    prior = pl.pallas_call(
        prior_kernel,
        out_shape=jax.ShapeDtypeStruct(fields.shape, f32),
        in_specs=[SMEM, SMEM] + [VMEM] * 4,
        out_specs=VMEM,
        cost_estimate=pl.CostEstimate(
            flops=20 * SWEEPS * fields.size, bytes_accessed=20 * fields.size, transcendentals=0
        ),
        name="prior",
    )(anisotropy, precision, fields, kappa_sq, from_low, from_high)

    grid_cells = float(rows * spaces * columns)
    return pl.pallas_call(
        lambda *refs: final_kernel(grid_cells, *refs),
        out_shape=jax.ShapeDtypeStruct(fields.shape, f32),
        in_specs=[VMEM] * 3,
        out_specs=VMEM,
        cost_estimate=pl.CostEstimate(flops=2 * fields.size, bytes_accessed=12 * fields.size, transcendentals=0),
        name="final",
    )(summed, cell_parts, prior)


def solution(mesh):
    return jax.shard_map(
        local,
        mesh=mesh,
        in_specs=(
            P("years", None, "space", None),
            P(None, "space", None),
            P(None, "space", None),
            P(),
            P(),
            P("space", None),
            P("years"),
            P("space", None),
        ),
        out_specs=P(None, "space", None),
        check_vma=False,
    )
```

time: 214 us -> 64.9 us (0.30)
  the two profiles are of different devices: /device:TPU:1 before, /device:TPU:8 now
where the time goes in v1:
time: 64.9 us; the launch traced here: 64.4 us
  starting transfers between devices  25.3 us (39%)
  blocking collectives  17.4 us (27%)
  waiting for transfers between devices  10.1 us (16%)
  Pallas kernels  9.65 us (15%)
  local copies, waits for them, and re-layouts  1.95 us (3%)
    all_to_all x1, blocking collectives, local(): parts = lax.all_to_all(tiles, 'years', 0, 0, tiled=True)  17.4 us
    all_to_all x1, starting transfers between devices, local(): cell_parts = lax.all_to_all(cells, 'space', 0, 0, tiled=True)  11.5 us
    all_to_all x1, waiting for transfers between devices, local(): cell_parts = lax.all_to_all(cells, 'space', 0, 0, tiled=True)  8.04 us
    ppermute x1, starting transfers between devices, local(): from_high = lax.ppermute(low, 'space', shifted('space', -1))  6.96 us
    all_to_all x1, starting transfers between devices, local(): lax.all_to_all(spread.reshape(tile_count, SUB, LANES), 'years', 0, 0, til...  4.93 us
    pallas_call x1, Pallas kernels, local(): pl.pallas_call(prior_kernel, out_shape=jax.ShapeDtypeStruct(fields.shape,...  3.6 us
    pallas_call x1, Pallas kernels, local(): pl.pallas_call(likelihood_kernel, out_shape=(tiles_shape, jax.ShapeDtypeS...  2.71 us
    unnamed x11, local copies, waits for them, and re-layouts  1.95 us
  transfers between devices with their start and end apart: 4, of which 3 were waited for; matrix products, arithmetic and copies ran while one was open for 1% of the time, Pallas kernels for 8%

profile of v1, /device:TPU:8, one launch (start us, length us, event | category | flops | bytes accessed | tf_op | source)
XLA Modules:
  0.0 64.4 jit_solution(12512719613344941208)
XLA Ops:
  0.0 0.0 copy-start.4
  0.0 2.7 %likelihood.1 = (f32[32,8,128]{2,1,0:T(8,128)}, f32[64,128]{1,0:T(8,128)}, f32[6,8,640]{2,1,0:T(8,128)}, f32[6,8,640]{2,1,0:T(8,128)}) custom-call(s32[4]{0:T(128)} %valid_ref.1, f32[4,8,16,640]{3,2,1,0:T(8,128)} %maxima_ref.1, f32[3,16,640]{2,1,0:T(8,128)} %fields_ref.3, f32[3,16,640]{2,1,0:T(8,128)} %kappa_ref.3, s32[16,640]{1,0:T(8,128)} %mask_ref.1, ...), custom_call_target="tpu_custom_call" | custom-call | flops 6553600 | bytes 1310720 | tf_op jit(solution)/shard_map/likelihood/pallas_call | solution.py:146
  2.7 17.4 %all_to_all.21 = f32[32,8,128]{2,1,0:T(8,128)} all-to-all(f32[32,8,128]{2,1,0:T(8,128)} %get-tuple-element.9), channel_id=1, replica_groups=mesh['space'=64,'years'=8] {'years'}, dimensions={0} | all-to-all | bytes 262144 | tf_op jit(solution)/shard_map/all_to_all | solution.py:157
  20.1 11.5 %all-to-all-start.2 = ((f32[64,1,128]{2,1,0:T(1,128)}), f32[64,1,128]{2,1,0:T(1,128)S(1)}, u32[]{:S(2)}, u32[]{:S(2)}) async-start(f32[64,1,128]{2,1,0:T(1,128)} %bitcast.9), calls=%async_computation.2 | async-start | bytes 65536 | tf_op jit(solution)/shard_map/all_to_all | solution.py:160
  31.6 1.6 %middle.1 = f32[8,4,8,128]{3,2,1,0:T(8,128)} custom-call(f32[8,4,8,128]{3,2,1,0:T(8,128)} %bitcast.7), custom_call_target="tpu_custom_call" | custom-call | flops 32768 | bytes 262144 | tf_op jit(solution)/shard_map/middle/pallas_call | solution.py:162
  33.2 8.0 %all-to-all-done.2 = f32[64,1,128]{2,1,0:T(1,128)S(1)} async-done(((f32[64,1,128]{2,1,0:T(1,128)}), f32[64,1,128]{2,1,0:T(1,128)S(1)}, u32[]{:S(2)}, u32[]{:S(2)}) %all-to-all-start.2) | async-done | bytes 32800 | tf_op jit(solution)/shard_map/all_to_all | solution.py:160
  41.2 0.0 copy-start.1
  41.2 4.9 %all-to-all-start.1 = ((f32[32,8,128]{2,1,0:T(8,128)}), f32[32,8,128]{2,1,0:T(8,128)S(1)}, u32[]{:S(2)}, u32[]{:S(2)}) async-start(f32[32,8,128]{2,1,0:T(8,128)} %bitcast.6), calls=%async_computation.1 | async-start | bytes 262144 | tf_op jit(solution)/shard_map/all_to_all | solution.py:170
  46.1 1.9 %collective-permute-start = (f32[6,8,640]{2,1,0:T(8,128)}, f32[6,8,640]{2,1,0:T(8,128)S(1)}, u32[]{:S(2)}, u32[]{:S(2)}) collective-permute-start(f32[6,8,640]{2,1,0:T(8,128)} %get-tuple-element.11), channel_id=1, source_target_pairs={{0,8},{8,16},{16,24},{24,32},{32,40},{40,48},{48,56},{56,64},{64,7... | collective-permute-start | bytes 368648 | tf_op jit(solution)/shard_map/ppermute | solution.py:158
  48.1 7.0 %collective-permute-start.1 = (f32[6,8,640]{2,1,0:T(8,128)}, f32[6,8,640]{2,1,0:T(8,128)S(1)}, u32[]{:S(2)}, u32[]{:S(2)}) collective-permute-start(f32[6,8,640]{2,1,0:T(8,128)} %get-tuple-element.12), channel_id=1, source_target_pairs={{0,504},{8,0},{16,8},{24,16},{32,24},{40,32},{48,40},{56,48},{64,5... | collective-permute-start | bytes 368648 | tf_op jit(solution)/shard_map/ppermute | solution.py:159
  55.0 0.0 copy-done.4
  55.0 0.7 %copy.11.aniso_ref = f32[3,2]{1,0:T(4,128)} copy(f32[3,2]{0,1:T(2,128)S(1)} %copy-done.4) | data formatting | bytes 48 | tf_op args[3]
  55.7 0.2 collective-permute-done.low_ref
  55.9 0.0 copy-start.2
  55.9 1.9 %collective-permute-done.1.high_ref = f32[6,8,640]{2,1,0:T(8,128)S(1)} collective-permute-done((f32[6,8,640]{2,1,0:T(8,128)}, f32[6,8,640]{2,1,0:T(8,128)S(1)}, u32[]{:S(2)}, u32[]{:S(2)}) %collective-permute-start.1) | collective-permute-done | bytes 122912 | tf_op jit(solution)/shard_map/ppermute | solution.py:159
  57.8 0.0 copy-done.2
  57.8 0.0 copy-start.3
  57.8 0.6 %copy-done.3 = f32[6,8,640]{2,1,0:T(8,128)} copy-done((f32[6,8,640]{2,1,0:T(8,128)}, f32[6,8,640]{2,1,0:T(8,128)S(1)}, u32[]{:S(2)}) %copy-start.3) | copy-done | bytes 122904
  58.4 3.6 %prior.1.refs_2_ = f32[3,16,640]{2,1,0:T(8,128)} custom-call(f32[3,2]{1,0:T(4,128)} %copy.11.aniso_ref, f32[3]{0:T(128)} %precision_ref.1, f32[3,16,640]{2,1,0:T(8,128)} %fields_ref.3, f32[3,16,640]{2,1,0:T(8,128)} %kappa_ref.3, f32[6,8,640]{2,1,0:T(8,128)} %copy-done.2, f32[6,8,640]{2,1,0:T(8,128)} %copy-done.3), custom_call_target="tpu_custom_call" | custom-call | flops 4915200 | bytes 614400 | tf_op jit(solution)/shard_map/prior/pallas_call | solution.py:174
  62.0 0.0 all-to-all-done.1.refs_0_
  62.0 0.0 copy-start
  62.0 0.0 copy-done.1
  62.0 0.6 copy-done
  62.7 1.8 %final.1 = f32[3,16,640]{2,1,0:T(8,128)} custom-call(f32[32,8,128]{2,1,0:T(8,128)} %copy-done, f32[64,128]{1,0:T(8,128)} %bitcast.8, f32[3,16,640]{2,1,0:T(8,128)} %prior.1.refs_2_), custom_call_target="tpu_custom_call" | custom-call | flops 61440 | bytes 368640 | tf_op jit(solution)/shard_map/final/pallas_call | solution.py:186
Async XLA Ops:
  0.0 55.0 %copy-start.4 = (f32[3,2]{0,1:T(2,128)S(1)}, f32[3,2]{0,1:T(2,128)}, u32[]{:S(2)}) copy-start(f32[3,2]{0,1:T(2,128)} %param.11) | copy-start | bytes 76
  20.1 21.1 %all-to-all-start.2 = ((f32[64,1,128]{2,1,0:T(1,128)}), f32[64,1,128]{2,1,0:T(1,128)S(1)}, u32[]{:S(2)}, u32[]{:S(2)}) async-start(f32[64,1,128]{2,1,0:T(1,128)} %bitcast.9), calls=%async_computation.2 | async-start | bytes 65536 | tf_op jit(solution)/shard_map/all_to_all | solution.py:160
  41.2 20.8 %copy-start.1 = (f32[64,1,128]{2,1,0:T(1,128)}, f32[64,1,128]{2,1,0:T(1,128)S(1)}, u32[]{:S(2)}) copy-start(f32[64,1,128]{2,1,0:T(1,128)S(1)} %all-to-all-done.2) | copy-start | bytes 98308
  41.2 20.8 %all-to-all-start.1 = ((f32[32,8,128]{2,1,0:T(8,128)}), f32[32,8,128]{2,1,0:T(8,128)S(1)}, u32[]{:S(2)}, u32[]{:S(2)}) async-start(f32[32,8,128]{2,1,0:T(8,128)} %bitcast.6), calls=%async_computation.1 | async-start | bytes 262144 | tf_op jit(solution)/shard_map/all_to_all | solution.py:170
  46.1 9.7 %collective-permute-start = (f32[6,8,640]{2,1,0:T(8,128)}, f32[6,8,640]{2,1,0:T(8,128)S(1)}, u32[]{:S(2)}, u32[]{:S(2)}) collective-permute-start(f32[6,8,640]{2,1,0:T(8,128)} %get-tuple-element.11), channel_id=1, source_target_pairs={{0,8},{8,16},{16,24},{24,32},{32,40},{40,48},{48,56},{56,64},{64,7... | collective-permute-start | bytes 368648 | tf_op jit(solution)/shard_map/ppermute | solution.py:158
  48.1 9.7 %collective-permute-start.1 = (f32[6,8,640]{2,1,0:T(8,128)}, f32[6,8,640]{2,1,0:T(8,128)S(1)}, u32[]{:S(2)}, u32[]{:S(2)}) collective-permute-start(f32[6,8,640]{2,1,0:T(8,128)} %get-tuple-element.12), channel_id=1, source_target_pairs={{0,504},{8,0},{16,8},{24,16},{32,24},{40,32},{48,40},{56,48},{64,5... | collective-permute-start | bytes 368648 | tf_op jit(solution)/shard_map/ppermute | solution.py:159
  55.9 1.9 %copy-start.2 = (f32[6,8,640]{2,1,0:T(8,128)}, f32[6,8,640]{2,1,0:T(8,128)S(1)}, u32[]{:S(2)}) copy-start(f32[6,8,640]{2,1,0:T(8,128)S(1)} %collective-permute-done.low_ref) | copy-start | bytes 368644
  57.8 0.6 %copy-start.3 = (f32[6,8,640]{2,1,0:T(8,128)}, f32[6,8,640]{2,1,0:T(8,128)S(1)}, u32[]{:S(2)}) copy-start(f32[6,8,640]{2,1,0:T(8,128)S(1)} %collective-permute-done.1.high_ref) | copy-start | bytes 368644
  62.0 0.6 copy-start

commit v2 on v1

--- a/solution.py
+++ b/solution.py
@@ -9,19 +9,50 @@
 HALO = 8
 LANES = 128
 SUB = 8
+MIB = 1 << 20
+PIECE = 4
+WIDE = 96
+CELL_LANE = 96
+YEAR_LANE = 97
 VMEM = pl.BlockSpec(memory_space=pltpu.VMEM)
 SMEM = pl.BlockSpec(memory_space=pltpu.SMEM)
 
 
+def packed_tiles(tiles, spare):
+    lane = lax.broadcasted_iota(jnp.int32, (SUB, LANES), 1)
+    packed = list(tiles[:24])
+    packed += [jnp.where(lane < WIDE, tile, spare) for tile in tiles[24:]]
+    for i in (24, 27):
+        rolled = [pltpu.roll(tiles[i + j], 32 * (j + 1), 1) for j in range(3)]
+        rest = jnp.where(lane < 32, rolled[0], jnp.where(lane < 64, rolled[1], rolled[2]))
+        packed.append(jnp.where(lane < WIDE, rest, spare))
+    return packed
+
+
+def unpacked_tiles(packed):
+    lane = lax.broadcasted_iota(jnp.int32, (SUB, LANES), 1)
+    tiles = list(packed[:24])
+    for i in range(6):
+        rest = pltpu.roll(packed[30 + i // 3], 96 - 32 * (i % 3), 1)
+        tiles.append(jnp.where(lane < WIDE, packed[24 + i], rest))
+    return tiles
+
+
+def place(q):
+    row, group = (q % 3, q // 3) if q < 24 else (3, q - 24)
+    return pl.ds(group * SUB * PIECE + row, SUB, PIECE)
+
+
 def likelihood_kernel(
     valid_ref, maxima_ref, fields_ref, kappa_ref, mask_ref, counts_ref,
-    tiles_ref, cells_ref, low_ref, high_ref,
+    packed_ref, cells_ref, low_ref, high_ref,
 ):
     years, orders, rows, columns = maxima_ref.shape
     row_tiles, lane_tiles = rows // SUB, columns // LANES
     valid = [valid_ref[t].astype(jnp.float32) for t in range(years)]
     valid_sum = sum(valid[1:], valid[0])
     cells = jnp.zeros((SUB, LANES), jnp.float32)
+    tiles = [None] * (3 * row_tiles * lane_tiles)
     for r in range(row_tiles):
         for c in range(lane_tiles):
             at = (pl.ds(r * SUB, SUB), pl.ds(c * LANES, LANES))
@@ -73,28 +104,20 @@
                 ) * inv_shape,
             )
             for f in range(3):
-                tiles_ref[(f * row_tiles + r) * lane_tiles + c] = grad[f] * mask
+                tiles[(f * row_tiles + r) * lane_tiles + c] = grad[f] * mask
             cells = cells + mask * count.astype(jnp.float32)
-    used_tiles = 3 * row_tiles * lane_tiles
-    tiles_ref[used_tiles] = jnp.full((SUB, LANES), valid_sum, jnp.float32)
-    for q in range(used_tiles + 1, tiles_ref.shape[0]):
-        tiles_ref[q] = jnp.zeros((SUB, LANES), jnp.float32)
-    cells_ref[...] = jnp.broadcast_to(
-        jnp.sum(cells, axis=0, keepdims=True), cells_ref.shape
-    )
+    lane = lax.broadcasted_iota(jnp.int32, (SUB, LANES), 1)
+    spare = jnp.where(lane == YEAR_LANE, valid_sum, 0.0)
+    for q, tile in enumerate(packed_tiles(tiles, spare)):
+        packed_ref[place(q), :] = tile
+    cell_sum = jnp.sum(jnp.sum(cells, axis=0, keepdims=True), axis=1, keepdims=True)
+    row = lax.broadcasted_iota(jnp.int32, (PIECE, LANES), 0)
+    lane = lax.broadcasted_iota(jnp.int32, (PIECE, LANES), 1)
+    cells_ref[...] = jnp.where((row == PIECE - 1) & (lane == CELL_LANE), cell_sum, 0.0)
     low_ref[0:3] = fields_ref[:, 0:HALO]
     low_ref[3:6] = kappa_ref[:, 0:HALO]
     high_ref[0:3] = fields_ref[:, rows - HALO : rows]
     high_ref[3:6] = kappa_ref[:, rows - HALO : rows]
-
-
-def middle_kernel(parts_ref, out_ref):
-    groups = parts_ref.shape[0]
-    total = parts_ref[0]
-    for g in range(1, groups):
-        total = total + parts_ref[g]
-    for g in range(groups):
-        out_ref[g] = total
 
 
 def prior_kernel(aniso_ref, precision_ref, fields_ref, kappa_ref, low_ref, high_ref, out_ref):
@@ -102,7 +125,7 @@
     extent = rows + 2 * HALO
     lane = lax.broadcasted_iota(jnp.int32, (extent, columns), 1)
     for f in range(3):
-        zonal, meridional = aniso_ref[f, 0], aniso_ref[f, 1]
+        zonal, meridional = aniso_ref[0, f], aniso_ref[1, f]
         values = jnp.concatenate([low_ref[f], fields_ref[f], high_ref[f]], axis=0)
         centre = jnp.concatenate([low_ref[3 + f], kappa_ref[f], high_ref[3 + f]], axis=0)
         centre = centre + (2.0 * zonal + 2.0 * meridional)
@@ -114,19 +137,25 @@
         out_ref[f] = precision_ref[f] * values[HALO : HALO + rows]
 
 
-def final_kernel(grid_cells, tiles_ref, cells_ref, prior_ref, out_ref):
+def final_kernel(grid_cells, packed_ref, prior_ref, out_ref):
     rows, columns = out_ref.shape[1:]
     row_tiles, lane_tiles = rows // SUB, columns // LANES
-    cell_count = jnp.sum(
-        jnp.sum(cells_ref[...], axis=0, keepdims=True), axis=1, keepdims=True
-    )
-    year_count = tiles_ref[3 * row_tiles * lane_tiles, 0:1, 0:1]
+    packed = [packed_ref[place(q), :] for q in range(32)]
+    spare = packed[24]
+    for tile in packed[25:]:
+        spare = spare + tile
+    spare = jnp.sum(spare, axis=0, keepdims=True)
+    lane = lax.broadcasted_iota(jnp.int32, spare.shape, 1)
+    cell_count = jnp.sum(jnp.where(lane == CELL_LANE, spare, 0.0), axis=1, keepdims=True)
+    years = jnp.where(lane == YEAR_LANE, packed[24][0:1], 0.0)
+    year_count = jnp.sum(years, axis=1, keepdims=True)
     scale = jnp.broadcast_to(grid_cells / (cell_count * year_count), (SUB, LANES))
+    tiles = unpacked_tiles(packed)
     for f in range(3):
         for r in range(row_tiles):
             for c in range(lane_tiles):
                 at = (f, pl.ds(r * SUB, SUB), pl.ds(c * LANES, LANES))
-                tile = tiles_ref[(f * row_tiles + r) * lane_tiles + c]
+                tile = tiles[(f * row_tiles + r) * lane_tiles + c]
                 out_ref[at] = tile * scale + prior_ref[at]
 
 
@@ -139,13 +168,17 @@
     f32 = jnp.float32
     rows, columns = fields.shape[1:]
     spaces, groups = lax.axis_size("space"), lax.axis_size("years")
-    used_tiles = 3 * (rows // SUB) * (columns // LANES) + 1
-    tile_count = -(-used_tiles // groups) * groups
-    tiles_shape = jax.ShapeDtypeStruct((tile_count, SUB, LANES), f32)
+    members = 8 * groups
+    planes = [[z * members + m for m in range(members)] for z in range(spaces // 8)]
     halo_shape = jax.ShapeDtypeStruct((6, HALO, columns), f32)
-    tiles, cells, low, high = pl.pallas_call(
+    packed, cells, low, high = pl.pallas_call(
         likelihood_kernel,
-        out_shape=(tiles_shape, jax.ShapeDtypeStruct((spaces, LANES), f32), halo_shape, halo_shape),
+        out_shape=(
+            jax.ShapeDtypeStruct((members * PIECE, LANES), f32),
+            jax.ShapeDtypeStruct((PIECE, LANES), f32),
+            halo_shape,
+            halo_shape,
+        ),
         in_specs=[SMEM] + [VMEM] * 5,
         out_specs=(VMEM,) * 4,
         cost_estimate=pl.CostEstimate(
@@ -154,22 +187,25 @@
         name="likelihood",
     )(year_valid, maxima, fields, kappa_sq, ocean_mask, counts)
 
-    parts = lax.all_to_all(tiles, "years", 0, 0, tiled=True)
+    def exchange(pieces):
+        return lax.all_to_all(
+            pieces, ("space", "years"), 0, 0, tiled=True, axis_index_groups=planes
+        )
+
+    parts = exchange(packed.reshape(members, PIECE, LANES))
+    far = [
+        (((z + y) % 8 * 8 + a) * groups + y, (z * 8 + a) * groups + y)
+        for z in range(8)
+        for a in range(8)
+        for y in range(groups)
+    ]
+    far_cells = lax.ppermute(cells, ("space", "years"), far)
+    summed = jnp.sum(parts.reshape(8, groups, PIECE, LANES), axis=1) + far_cells
+    spread = jnp.broadcast_to(summed[:, None], (8, groups, PIECE, LANES))
+    spread, low, high = lax.optimization_barrier((spread, low, high))
     from_low = lax.ppermute(high, "space", shifted("space", 1))
     from_high = lax.ppermute(low, "space", shifted("space", -1))
-    cell_parts = lax.all_to_all(cells, "space", 0, 0, tiled=True)
-
-    spread = pl.pallas_call(
-        middle_kernel,
-        out_shape=jax.ShapeDtypeStruct((groups, tile_count // groups, SUB, LANES), f32),
-        in_specs=[VMEM],
-        out_specs=VMEM,
-        cost_estimate=pl.CostEstimate(flops=tiles.size, bytes_accessed=8 * tiles.size, transcendentals=0),
-        name="middle",
-    )(parts.reshape(groups, tile_count // groups, SUB, LANES))
-    summed = lax.all_to_all(
-        spread.reshape(tile_count, SUB, LANES), "years", 0, 0, tiled=True
-    )
+    whole = exchange(spread.reshape(members, PIECE, LANES))
 
     prior = pl.pallas_call(
         prior_kernel,
@@ -179,18 +215,20 @@
         cost_estimate=pl.CostEstimate(
             flops=20 * SWEEPS * fields.size, bytes_accessed=20 * fields.size, transcendentals=0
         ),
+        compiler_params=pltpu.CompilerParams(vmem_limit_bytes=6 * MIB),
         name="prior",
-    )(anisotropy, precision, fields, kappa_sq, from_low, from_high)
+    )(anisotropy.T, precision, fields, kappa_sq, from_low, from_high)
 
     grid_cells = float(rows * spaces * columns)
     return pl.pallas_call(
         lambda *refs: final_kernel(grid_cells, *refs),
         out_shape=jax.ShapeDtypeStruct(fields.shape, f32),
-        in_specs=[VMEM] * 3,
+        in_specs=[VMEM] * 2,
         out_specs=VMEM,
         cost_estimate=pl.CostEstimate(flops=2 * fields.size, bytes_accessed=12 * fields.size, transcendentals=0),
+        compiler_params=pltpu.CompilerParams(vmem_limit_bytes=3 * MIB),
         name="final",
-    )(summed, cell_parts, prior)
+    )(whole.reshape(members * PIECE, LANES), prior)
 
 
 def solution(mesh):

time: 64.9 us -> 55.2 us (0.85)
  starting transfers between devices: 25.3 us -> 43.9 us
  blocking collectives: 17.4 us -> 0 us
  waiting for transfers between devices: 10.1 us -> 4.2 us
  Pallas kernels: 9.65 us -> 5.91 us
  local copies, waits for them, and re-layouts: 1.95 us -> 0.68 us
    all_to_all x1 -> x0, blocking collectives: 17.4 us -> none  [local(): parts = lax.all_to_all(tiles, 'years', 0, 0, tiled=True)]
    ppermute x0 -> x1, starting transfers between devices: none -> 10.9 us  [local(): far_cells = lax.ppermute(cells, ('space', 'years'), far)]
    all_to_all x2, waiting for transfers between devices: 8.05 us -> 0.01 us  [exchange(): lax.all_to_all(pieces, ('space', 'years'), 0, 0, tiled=True, axis_index_g...]
    all_to_all x2, starting transfers between devices: 16.4 us -> 21.1 us  [exchange(): lax.all_to_all(pieces, ('space', 'years'), 0, 0, tiled=True, axis_index_g...]
    ppermute x1, starting transfers between devices: 6.96 us -> 9.82 us  [local(): from_high = lax.ppermute(low, 'space', shifted('space', -1))]
    unnamed x11 -> x9, local copies, waits for them, and re-layouts: 1.95 us -> 0.02 us
    pallas_call x2 -> x1, Pallas kernels: 4.27 us -> 2.73 us  [local(): pl.pallas_call(likelihood_kernel, out_shape=(jax.ShapeDtypeStruct((member...]
    ppermute x0 -> x1, waiting for transfers between devices: none -> 1.46 us  [local(): far_cells = lax.ppermute(cells, ('space', 'years'), far)]
  transfers between devices with their start and end apart: 4 -> 5, of which waited for: 3 -> 3; matrix products, arithmetic and copies ran while one was open for 1% -> 0% of each run, Pallas kernels for 8% -> 4%
where the time goes in v2:
time: 55.2 us; the launch traced here: 54.8 us
  starting transfers between devices  43.9 us (80%)
  Pallas kernels  5.91 us (11%)
  waiting for transfers between devices  4.2 us (8%)
  local copies, waits for them, and re-layouts  0.68 us (1%)
    all_to_all x2, starting transfers between devices, exchange(): lax.all_to_all(pieces, ('space', 'years'), 0, 0, tiled=True, axis_index_g...  21.1 us
    ppermute x1, starting transfers between devices, local(): far_cells = lax.ppermute(cells, ('space', 'years'), far)  10.9 us
    ppermute x1, starting transfers between devices, local(): from_high = lax.ppermute(low, 'space', shifted('space', -1))  9.82 us
    pallas_call x1, Pallas kernels, local(): pl.pallas_call(likelihood_kernel, out_shape=(jax.ShapeDtypeStruct((member...  2.73 us
    pallas_call x1, Pallas kernels, local(): pl.pallas_call(prior_kernel, out_shape=jax.ShapeDtypeStruct(fields.shape,...  2.42 us
    ppermute x1, starting transfers between devices, local(): from_low = lax.ppermute(high, 'space', shifted('space', 1))  2.06 us
    ppermute x1, waiting for transfers between devices, local(): from_high = lax.ppermute(low, 'space', shifted('space', -1))  1.91 us
    ppermute x1, waiting for transfers between devices, local(): far_cells = lax.ppermute(cells, ('space', 'years'), far)  1.46 us
  transfers between devices with their start and end apart: 5, of which 3 were waited for; matrix products, arithmetic and copies ran while one was open for 0% of the time, Pallas kernels for 4%

profile of v2, /device:TPU:8, one launch (start us, length us, event | category | flops | bytes accessed | tf_op | source)
XLA Modules:
  0.0 54.8 jit_solution(10946843150040983785)
XLA Ops:
  0.0 0.0 copy-start.1
  0.0 0.0 copy-start
  0.0 0.0 copy-start.3
  0.0 0.0 copy-start.2
  0.0 2.7 %likelihood.1 = (f32[256,128]{1,0:T(8,128)}, f32[4,128]{1,0:T(4,128)}, f32[6,8,640]{2,1,0:T(8,128)}, f32[6,8,640]{2,1,0:T(8,128)}) custom-call(s32[4]{0:T(128)} %valid_ref.1, f32[4,8,16,640]{3,2,1,0:T(8,128)} %maxima_ref.1, f32[3,16,640]{2,1,0:T(8,128)} %fields_ref.3, f32[3,16,640]{2,1,0:T(8,128)} %kappa_ref.3, s32[16,640]{1,0:T(8,128)} %mask_ref.1, ...), custom_call_target="tpu_custom_call" | custom-call | flops 6553600 | bytes 1310720 | tf_op jit(solution)/shard_map/likelihood/pallas_call | solution.py:174
  2.7 10.6 %all-to-all-start = ((f32[64,4,128]{2,1,0:T(4,128)}), f32[64,4,128]{2,1,0:T(4,128)S(1)}, u32[]{:S(2)}, u32[]{:S(2)}) async-start(f32[64,4,128]{2,1,0:T(4,128)} %bitcast.11), calls=%async_computation | async-start | bytes 262144 | tf_op jit(solution)/shard_map/all_to_all | solution.py:191
  13.3 10.9 %collective-permute-start = (f32[4,128]{1,0:T(4,128)}, f32[4,128]{1,0:T(4,128)S(1)}, u32[]{:S(2)}, u32[]{:S(2)}) collective-permute-start(f32[4,128]{1,0:T(4,128)} %get-tuple-element.13), channel_id=1, source_target_pairs={{0,0},{65,1},{130,2},{195,3},{260,4},{325,5},{390,6},{455,7},{8,8}... | collective-permute-start | bytes 6152 | tf_op jit(solution)/shard_map/ppermute | solution.py:202
  24.3 0.0 all-to-all-done
  24.3 1.5 %collective-permute-done = f32[4,128]{1,0:T(4,128)S(1)} collective-permute-done((f32[4,128]{1,0:T(4,128)}, f32[4,128]{1,0:T(4,128)S(1)}, u32[]{:S(2)}, u32[]{:S(2)}) %collective-permute-start) | collective-permute-done | bytes 2080 | tf_op jit(solution)/shard_map/ppermute | solution.py:202
  25.8 0.7 %broadcast_in_dim.2 = f32[8,8,4,128]{3,2,1,0:T(4,128)} broadcast(f32[8,4,128]{2,1,0:T(4,128)S(1)} %bitcast.13), dimensions={0,2,3} | broadcast | bytes 147456 | tf_op jit(solution)/shard_map/broadcast_in_dim | solution.py:204
  26.5 10.5 %all-to-all-start.1 = ((f32[64,4,128]{2,1,0:T(4,128)}), f32[64,4,128]{2,1,0:T(4,128)S(1)}, u32[]{:S(2)}, u32[]{:S(2)}) async-start(f32[64,4,128]{2,1,0:T(4,128)} %bitcast.2), calls=%async_computation.1 | async-start | bytes 262144 | tf_op jit(solution)/shard_map/all_to_all | solution.py:191
  37.0 2.1 %collective-permute-start.1 = (f32[6,8,640]{2,1,0:T(8,128)}, f32[6,8,640]{2,1,0:T(8,128)S(1)}, u32[]{:S(2)}, u32[]{:S(2)}) collective-permute-start(f32[6,8,640]{2,1,0:T(8,128)} %get-tuple-element.17), channel_id=1, source_target_pairs={{0,8},{8,16},{16,24},{24,32},{32,40},{40,48},{48,56},{56,64},{64,7... | collective-permute-start | bytes 368648 | tf_op jit(solution)/shard_map/ppermute | solution.py:206
  39.0 9.8 %collective-permute-start.2 = (f32[6,8,640]{2,1,0:T(8,128)}, f32[6,8,640]{2,1,0:T(8,128)S(1)}, u32[]{:S(2)}, u32[]{:S(2)}) collective-permute-start(f32[6,8,640]{2,1,0:T(8,128)} %get-tuple-element.18), channel_id=1, source_target_pairs={{0,504},{8,0},{16,8},{24,16},{32,24},{40,32},{48,40},{56,48},{64,5... | collective-permute-start | bytes 368648 | tf_op jit(solution)/shard_map/ppermute | solution.py:207
  48.9 0.8 %collective-permute-done.1.low_ref = f32[6,8,640]{2,1,0:T(8,128)S(1)} collective-permute-done((f32[6,8,640]{2,1,0:T(8,128)}, f32[6,8,640]{2,1,0:T(8,128)S(1)}, u32[]{:S(2)}, u32[]{:S(2)}) %collective-permute-start.1) | collective-permute-done | bytes 122912 | tf_op jit(solution)/shard_map/ppermute | solution.py:206
  49.7 1.9 %collective-permute-done.2.high_ref = f32[6,8,640]{2,1,0:T(8,128)S(1)} collective-permute-done((f32[6,8,640]{2,1,0:T(8,128)}, f32[6,8,640]{2,1,0:T(8,128)S(1)}, u32[]{:S(2)}, u32[]{:S(2)}) %collective-permute-start.2) | collective-permute-done | bytes 122912 | tf_op jit(solution)/shard_map/ppermute | solution.py:207
  51.6 0.0 copy-done.1
  51.6 0.0 copy-done
  51.6 0.0 copy-done.3
  51.6 0.0 copy-done.2
  51.6 2.4 %prior.1.refs_1_ = f32[3,16,640]{2,1,0:T(8,128)S(1)} custom-call(f32[2,3]{1,0:T(2,128)S(1)} %bitcast.10, f32[3]{0:T(128)S(1)} %copy-done.3, f32[3,16,640]{2,1,0:T(8,128)S(1)} %copy-done, f32[3,16,640]{2,1,0:T(8,128)S(1)} %copy-done.1, f32[6,8,640]{2,1,0:T(8,128)S(1)} %collective-permute-done.1.low_ref, f32[6,8,640]{2,1,0:T(8,128)S(1)} %collective-permute-done.2.high_ref), custom_call_target="tpu_custom_call" | custom-call | flops 4915200 | bytes 614400 | tf_op jit(solution)/shard_map/prior/pallas_call | solution.py:210
  54.1 0.0 all-to-all-done.1
  54.1 0.8 %final.1 = f32[3,16,640]{2,1,0:T(8,128)} custom-call(f32[256,128]{1,0:T(8,128)S(1)} %bitcast.9, f32[3,16,640]{2,1,0:T(8,128)S(1)} %prior.1.refs_1_), custom_call_target="tpu_custom_call" | custom-call | flops 61440 | bytes 368640 | tf_op jit(solution)/shard_map/final/pallas_call | solution.py:223
  (3 shorter events, 0.0 us)
Async XLA Ops:
  0.0 51.6 %copy-start.1 = (f32[3,16,640]{2,1,0:T(8,128)S(1)}, f32[3,16,640]{2,1,0:T(8,128)}, u32[]{:S(2)}) copy-start(f32[3,16,640]{2,1,0:T(8,128)} %kappa_ref.3) | copy-start | bytes 368644
  0.0 51.6 %copy-start = (f32[3,16,640]{2,1,0:T(8,128)S(1)}, f32[3,16,640]{2,1,0:T(8,128)}, u32[]{:S(2)}) copy-start(f32[3,16,640]{2,1,0:T(8,128)} %fields_ref.3) | copy-start | bytes 368644
  0.0 51.6 %copy-start.3 = (f32[3]{0:T(128)S(1)}, f32[3]{0:T(128)}, u32[]{:S(2)}) copy-start(f32[3]{0:T(128)} %precision_ref.1) | copy-start | bytes 40
  0.0 51.6 %copy-start.2 = (f32[3,2]{0,1:T(2,128)S(1)}, f32[3,2]{0,1:T(2,128)}, u32[]{:S(2)}) copy-start(f32[3,2]{0,1:T(2,128)} %param.11) | copy-start | bytes 76
  2.7 21.5 %all-to-all-start = ((f32[64,4,128]{2,1,0:T(4,128)}), f32[64,4,128]{2,1,0:T(4,128)S(1)}, u32[]{:S(2)}, u32[]{:S(2)}) async-start(f32[64,4,128]{2,1,0:T(4,128)} %bitcast.11), calls=%async_computation | async-start | bytes 262144 | tf_op jit(solution)/shard_map/all_to_all | solution.py:191
  13.3 12.5 %collective-permute-start = (f32[4,128]{1,0:T(4,128)}, f32[4,128]{1,0:T(4,128)S(1)}, u32[]{:S(2)}, u32[]{:S(2)}) collective-permute-start(f32[4,128]{1,0:T(4,128)} %get-tuple-element.13), channel_id=1, source_target_pairs={{0,0},{65,1},{130,2},{195,3},{260,4},{325,5},{390,6},{455,7},{8,8}... | collective-permute-start | bytes 6152 | tf_op jit(solution)/shard_map/ppermute | solution.py:202
  26.5 27.6 %all-to-all-start.1 = ((f32[64,4,128]{2,1,0:T(4,128)}), f32[64,4,128]{2,1,0:T(4,128)S(1)}, u32[]{:S(2)}, u32[]{:S(2)}) async-start(f32[64,4,128]{2,1,0:T(4,128)} %bitcast.2), calls=%async_computation.1 | async-start | bytes 262144 | tf_op jit(solution)/shard_map/all_to_all | solution.py:191
  37.0 12.7 %collective-permute-start.1 = (f32[6,8,640]{2,1,0:T(8,128)}, f32[6,8,640]{2,1,0:T(8,128)S(1)}, u32[]{:S(2)}, u32[]{:S(2)}) collective-permute-start(f32[6,8,640]{2,1,0:T(8,128)} %get-tuple-element.17), channel_id=1, source_target_pairs={{0,8},{8,16},{16,24},{24,32},{32,40},{40,48},{48,56},{56,64},{64,7... | collective-permute-start | bytes 368648 | tf_op jit(solution)/shard_map/ppermute | solution.py:206
  39.0 12.6 %collective-permute-start.2 = (f32[6,8,640]{2,1,0:T(8,128)}, f32[6,8,640]{2,1,0:T(8,128)S(1)}, u32[]{:S(2)}, u32[]{:S(2)}) collective-permute-start(f32[6,8,640]{2,1,0:T(8,128)} %get-tuple-element.18), channel_id=1, source_target_pairs={{0,504},{8,0},{16,8},{24,16},{32,24},{40,32},{48,40},{56,48},{64,5... | collective-permute-start | bytes 368648 | tf_op jit(solution)/shard_map/ppermute | solution.py:207

commit v3 on v1

v3 whole, which is shorter than its diff:
```python
import jax
import jax.numpy as jnp
from jax import lax
from jax.experimental import pallas as pl
from jax.experimental.pallas import tpu as pltpu
from jax.sharding import PartitionSpec as P

SWEEPS = 8
HALO = 8
LANES = 128
SUB = 8
MIB = 1 << 20
PIECE = 32
CELL_ROW = 30
YEAR_ROW = 31
VMEM = pl.BlockSpec(memory_space=pltpu.VMEM)
SMEM = pl.BlockSpec(memory_space=pltpu.SMEM)


def place(q):
    if q < 24:
        return pl.ds(q // 3 * PIECE + q % 3 * SUB, SUB)
    return pl.ds(q, SUB, PIECE)


def cells_kernel(mask_ref, counts_ref, cells_ref):
    rows, columns = mask_ref.shape
    total = jnp.zeros((SUB, LANES), jnp.int32)
    for r in range(0, rows, SUB):
        for c in range(0, columns, LANES):
            at = (pl.ds(r, SUB), pl.ds(c, LANES))
            total = total + mask_ref[at] * counts_ref[at]
    total = jnp.sum(total.astype(jnp.float32), axis=0, keepdims=True)
    cells_ref[...] = jnp.broadcast_to(total, cells_ref.shape)


def likelihood_kernel(
    odd_ref, valid_ref, maxima_ref, fields_ref, kappa_ref, mask_ref, counts_ref,
    packed_ref, inner_ref, outer_ref,
):
    years, orders, rows, columns = maxima_ref.shape
    row_tiles, lane_tiles = rows // SUB, columns // LANES
    valid = [valid_ref[t].astype(jnp.float32) for t in range(years)]
    valid_sum = sum(valid[1:], valid[0])
    tiles = [None] * (3 * row_tiles * lane_tiles)
    for r in range(row_tiles):
        for c in range(lane_tiles):
            at = (pl.ds(r * SUB, SUB), pl.ds(c * LANES, LANES))
            location = fields_ref[(0,) + at]
            log_scale = fields_ref[(1,) + at]
            shape = fields_ref[(2,) + at]
            count = counts_ref[at]
            mask = mask_ref[at].astype(jnp.float32)
            inv_scale = jnp.exp(-log_scale)
            inv_shape = 1.0 / shape
            slope = shape * inv_scale
            sum_inv = jnp.zeros((SUB, LANES), jnp.float32)
            sum_log = jnp.zeros((SUB, LANES), jnp.float32)
            tail_sum = jnp.zeros((SUB, LANES), jnp.float32)
            tail_inv = jnp.zeros((SUB, LANES), jnp.float32)
            tail_log = jnp.zeros((SUB, LANES), jnp.float32)
            for t in range(years):
                inv_t = None
                for k in range(orders):
                    reduced = 1.0 + slope * (maxima_ref[(t, k) + at] - location)
                    if k == 0:
                        used, last = reduced, reduced
                    else:
                        is_used = count > k
                        used = jnp.where(is_used, reduced, 1.0)
                        last = jnp.where(is_used, reduced, last)
                    inv = 1.0 - 1.0 / used
                    log = jnp.log(used)
                    if k == 0:
                        inv_t, log_t = inv, log
                    else:
                        inv_t, log_t = inv_t + inv, log_t + log
                last_log = jnp.log(last)
                tail = jnp.exp(-last_log * inv_shape) * valid[t]
                sum_inv = sum_inv + inv_t * valid[t]
                sum_log = sum_log + log_t * valid[t]
                tail_sum = tail_sum + tail
                tail_inv = tail_inv + tail / last
                tail_log = tail_log + tail * last_log
            used_total = valid_sum * count.astype(jnp.float32)
            one_more = 1.0 + inv_shape
            tail_diff = tail_sum - tail_inv
            grad = (
                (tail_inv - (1.0 + shape) * (used_total - sum_inv)) * inv_scale,
                used_total - one_more * sum_inv + tail_diff * inv_shape,
                (
                    (tail_log - sum_log - tail_diff) * inv_shape
                    + one_more * sum_inv
                ) * inv_shape,
            )
            for f in range(3):
                tiles[(f * row_tiles + r) * lane_tiles + c] = grad[f] * mask
    for q, tile in enumerate(tiles):
        packed_ref[place(q), :] = tile
    packed_ref[pl.ds(CELL_ROW, SUB, PIECE), :] = jnp.zeros((SUB, LANES), jnp.float32)
    packed_ref[pl.ds(YEAR_ROW, SUB, PIECE), :] = jnp.full((SUB, LANES), valid_sum, jnp.float32)
    inner_row = pl.multiple_of((1 - odd_ref[0]) * (rows - HALO), HALO)
    outer_row = pl.multiple_of(odd_ref[0] * (rows - HALO), HALO)
    inner_ref[0:3] = fields_ref[:, pl.ds(inner_row, HALO)]
    inner_ref[3:6] = kappa_ref[:, pl.ds(inner_row, HALO)]
    outer_ref[0:3] = fields_ref[:, pl.ds(outer_row, HALO)]
    outer_ref[3:6] = kappa_ref[:, pl.ds(outer_row, HALO)]


def prior_kernel(
    odd_ref, aniso_ref, precision_ref, fields_ref, kappa_ref, inner_ref, outer_ref, out_ref
):
    rows, columns = fields_ref.shape[1:]
    extent = rows + 2 * HALO
    lane = lax.broadcasted_iota(jnp.int32, (extent, columns), 1)
    odd = odd_ref[0] == 1

    def between(inner, rows_here, outer):
        low, high = jnp.where(odd, inner, outer), jnp.where(odd, outer, inner)
        return jnp.concatenate([low, rows_here, high], axis=0)

    for f in range(3):
        zonal, meridional = aniso_ref[0, f], aniso_ref[1, f]
        values = between(inner_ref[f], fields_ref[f], outer_ref[f])
        centre = between(inner_ref[3 + f], kappa_ref[f], outer_ref[3 + f])
        centre = centre + (2.0 * zonal + 2.0 * meridional)
        for _ in range(SWEEPS):
            east_west = pltpu.roll(values, 1, 0) + pltpu.roll(values, extent - 1, 0)
            south = jnp.where(lane == 0, 0.0, pltpu.roll(values, 1, 1))
            north = jnp.where(lane == columns - 1, 0.0, pltpu.roll(values, columns - 1, 1))
            values = centre * values - zonal * east_west - meridional * (south + north)
        out_ref[f] = precision_ref[f] * values[HALO : HALO + rows]


def middle_kernel(parts_ref, cells_ref, out_ref):
    groups = parts_ref.shape[0] // PIECE
    cells = jnp.sum(cells_ref[...], axis=0, keepdims=True)
    for i in range(0, PIECE, SUB):
        total = parts_ref[pl.ds(i, SUB), :]
        for g in range(1, groups):
            total = total + parts_ref[pl.ds(g * PIECE + i, SUB), :]
        if i <= CELL_ROW < i + SUB:
            row = lax.broadcasted_iota(jnp.int32, (SUB, LANES), 0)
            total = total + jnp.where(row == CELL_ROW - i, cells, 0.0)
        for g in range(groups):
            out_ref[pl.ds(g * PIECE + i, SUB), :] = total


def final_kernel(grid_cells, packed_ref, prior_ref, out_ref):
    rows, columns = out_ref.shape[1:]
    row_tiles, lane_tiles = rows // SUB, columns // LANES
    cells = jnp.sum(packed_ref[pl.ds(CELL_ROW, SUB, PIECE), :], axis=0, keepdims=True)
    cells = jnp.sum(cells, axis=1, keepdims=True)
    years = packed_ref[pl.ds(YEAR_ROW, 1), :]
    scale = grid_cells / (jnp.broadcast_to(cells, (SUB, LANES)) * years)
    for f in range(3):
        for r in range(row_tiles):
            for c in range(lane_tiles):
                at = (f, pl.ds(r * SUB, SUB), pl.ds(c * LANES, LANES))
                tile = packed_ref[place((f * row_tiles + r) * lane_tiles + c), :]
                out_ref[at] = tile * scale + prior_ref[at]


def local(maxima, fields, kappa_sq, anisotropy, precision, ocean_mask, year_valid, counts):
    f32 = jnp.float32
    rows, columns = fields.shape[1:]
    spaces, groups = lax.axis_size("space"), lax.axis_size("years")
    planes = [list(range(z, z + SUB)) for z in range(0, spaces, SUB)]
    cells = pl.pallas_call(
        cells_kernel,
        out_shape=jax.ShapeDtypeStruct((SUB, LANES), f32),
        in_specs=[VMEM] * 2,
        out_specs=VMEM,
        cost_estimate=pl.CostEstimate(flops=2 * ocean_mask.size, bytes_accessed=8 * ocean_mask.size, transcendentals=0),
        name="cells",
    )(ocean_mask, counts)
    plane_cells = lax.all_to_all(
        cells[:, None], "space", 0, 0, tiled=True, axis_index_groups=planes
    )[:, 0]

    odd = (lax.axis_index("space") % 2).astype(jnp.int32).reshape(1)
    halo_shape = jax.ShapeDtypeStruct((6, HALO, columns), f32)
    packed_shape = jax.ShapeDtypeStruct((groups * PIECE, LANES), f32)
    packed, inner, outer = pl.pallas_call(
        likelihood_kernel,
        out_shape=(packed_shape, halo_shape, halo_shape),
        in_specs=[SMEM] * 2 + [VMEM] * 5,
        out_specs=(VMEM,) * 3,
        cost_estimate=pl.CostEstimate(flops=10**11, bytes_accessed=1024 * MIB, transcendentals=0),
        name="likelihood",
    )(odd, year_valid, maxima, fields, kappa_sq, ocean_mask, counts)

    def exchange(pieces):
        pieces = pieces.reshape(groups, PIECE, LANES)
        pieces = lax.all_to_all(pieces, "years", 0, 0, tiled=True)
        return pieces.reshape(groups * PIECE, LANES)

    parts = exchange(packed)
    far = [
        (((z ^ y ^ 4) * SUB + a) * groups + y, (z * SUB + a) * groups + y)
        for z in range(spaces // SUB)
        for a in range(SUB)
        for y in range(groups)
    ]
    far_cells = lax.ppermute(plane_cells, ("space", "years"), far)
    spread = pl.pallas_call(
        middle_kernel,
        out_shape=packed_shape,
        in_specs=[VMEM] * 2,
        out_specs=VMEM,
        cost_estimate=pl.CostEstimate(flops=10**11, bytes_accessed=1024 * MIB, transcendentals=0),
        compiler_params=pltpu.CompilerParams(vmem_limit_bytes=3 * MIB),
        name="middle",
    )(parts, far_cells)
    from_inner = lax.ppermute(inner, "space", [(s, s ^ 1) for s in range(spaces)])
    outer_pairs = [(s, (s + (1 if s % 2 else -1)) % spaces) for s in range(spaces)]
    from_outer = lax.ppermute(outer, "space", outer_pairs)
    whole = exchange(spread)

    prior = pl.pallas_call(
        prior_kernel,
        out_shape=jax.ShapeDtypeStruct(fields.shape, f32),
        in_specs=[SMEM] * 3 + [VMEM] * 4,
        out_specs=VMEM,
        cost_estimate=pl.CostEstimate(
            flops=10**11, bytes_accessed=1024 * MIB, transcendentals=0
        ),
        compiler_params=pltpu.CompilerParams(vmem_limit_bytes=6 * MIB),
        name="prior",
    )(odd, anisotropy.T, precision, fields, kappa_sq, from_inner, from_outer)

    grid_cells = float(rows * spaces * columns)
    return pl.pallas_call(
        lambda *refs: final_kernel(grid_cells, *refs),
        out_shape=jax.ShapeDtypeStruct(fields.shape, f32),
        in_specs=[VMEM] * 2,
        out_specs=VMEM,
        cost_estimate=pl.CostEstimate(flops=2 * fields.size, bytes_accessed=12 * fields.size, transcendentals=0),
        compiler_params=pltpu.CompilerParams(vmem_limit_bytes=3 * MIB),
        name="final",
    )(whole, prior)


def solution(mesh):
    return jax.shard_map(
        local,
        mesh=mesh,
        in_specs=(
            P("years", None, "space", None),
            P(None, "space", None),
            P(None, "space", None),
            P(),
            P(),
            P("space", None),
            P("years"),
            P("space", None),
        ),
        out_specs=P(None, "space", None),
        check_vma=False,
    )
```

time: 64.9 us -> 50.5 us (0.78)
  blocking collectives: 17.4 us -> 0 us
  starting transfers between devices: 25.3 us -> 34.2 us
  waiting for transfers between devices: 10.1 us -> 7.68 us
  local copies, waits for them, and re-layouts: 1.95 us -> 0.03 us
  Pallas kernels: 9.65 us -> 7.99 us
    all_to_all x1 -> x0, blocking collectives: 17.4 us -> none  [local(): parts = lax.all_to_all(tiles, 'years', 0, 0, tiled=True)]
    ppermute x2 -> x3, starting transfers between devices: 8.87 us -> 15 us  [the longest x1 10.5 us: local(): far_cells = lax.ppermute(plane_cells, ('space', 'years'), far)]
    all_to_all x2 -> x3, starting transfers between devices: 16.4 us -> 19.1 us  [the longest x2 14.8 us: exchange(): pieces = lax.all_to_all(pieces, 'years', 0, 0, tiled=True)]
    ppermute x2 -> x3, waiting for transfers between devices: 2.06 us -> 0.01 us  [the longest x1 0.01 us: local(): far_cells = lax.ppermute(plane_cells, ('space', 'years'), far)]
    unnamed x11 -> x8, local copies, waits for them, and re-layouts: 1.95 us -> 0.03 us
    pallas_call x1, Pallas kernels: 3.6 us -> 2.42 us  [local(): pl.pallas_call(prior_kernel, out_shape=jax.ShapeDtypeStruct(fields.shape,...]
    pallas_call x1, Pallas kernels: 1.77 us -> 0.76 us  [local(): pl.pallas_call(lambda *refs: final_kernel(grid_cells, *refs), out_shape=j...]
    pallas_call x2 -> x3, Pallas kernels: 4.27 us -> 4.82 us  [the longest x1 2.74 us: local(): pl.pallas_call(likelihood_kernel, out_shape=(packed_shape, halo_shape, ha...]
  transfers between devices with their start and end apart: 4 -> 6, of which waited for: 3 -> 2; matrix products, arithmetic and copies ran while one was open for 1% -> 0% of each run, Pallas kernels for 8% -> 12%
where the time goes in v3:
time: 50.5 us; the launch traced here: 50 us
  starting transfers between devices  34.2 us (68%)
  Pallas kernels  7.99 us (16%)
  waiting for transfers between devices  7.68 us (15%)
    all_to_all x2, starting transfers between devices, exchange(): pieces = lax.all_to_all(pieces, 'years', 0, 0, tiled=True)  14.8 us
    ppermute x1, starting transfers between devices, local(): far_cells = lax.ppermute(plane_cells, ('space', 'years'), far)  10.5 us
    all_to_all x2, waiting for transfers between devices, exchange(): pieces = lax.all_to_all(pieces, 'years', 0, 0, tiled=True)  5.15 us
    all_to_all x1, starting transfers between devices, local(): lax.all_to_all(cells[:, None], 'space', 0, 0, tiled=True, axis_index_grou...  4.3 us
    pallas_call x1, Pallas kernels, local(): pl.pallas_call(likelihood_kernel, out_shape=(packed_shape, halo_shape, ha...  2.74 us
    ppermute x1, starting transfers between devices, local(): from_outer = lax.ppermute(outer, 'space', outer_pairs)  2.65 us
    all_to_all x1, waiting for transfers between devices, local(): lax.all_to_all(cells[:, None], 'space', 0, 0, tiled=True, axis_index_grou...  2.52 us
    pallas_call x1, Pallas kernels, local(): pl.pallas_call(prior_kernel, out_shape=jax.ShapeDtypeStruct(fields.shape,...  2.42 us
  transfers between devices with their start and end apart: 6, of which 2 were waited for; matrix products, arithmetic and copies ran while one was open for 0% of the time, Pallas kernels for 12%

profile of v3, /device:TPU:8, one launch (start us, length us, event | category | flops | bytes accessed | tf_op | source)
XLA Modules:
  0.0 50.0 jit_solution(11245005443503376964)
XLA Ops:
  0.0 1.4 %cells.1 = f32[8,128]{1,0:T(8,128)} custom-call(s32[16,640]{1,0:T(8,128)} %mask_ref.3, s32[16,640]{1,0:T(8,128)} %counts_ref.3), custom_call_target="tpu_custom_call" | custom-call | flops 20480 | bytes 81920 | tf_op jit(solution)/shard_map/cells/pallas_call | solution.py:169
  1.4 4.3 %all-to-all-start.1 = ((f32[8,1,128]{2,1,0:T(1,128)}), f32[8,1,128]{2,1,0:T(1,128)S(1)}, u32[]{:S(2)}, u32[]{:S(2)}) async-start(f32[8,1,128]{2,1,0:T(1,128)} %bitcast.14), calls=%async_computation.1 | async-start | bytes 8192 | tf_op jit(solution)/shard_map/all_to_all | solution.py:177
  5.7 2.7 %likelihood.1 = (f32[256,128]{1,0:T(8,128)}, f32[6,8,640]{2,1,0:T(8,128)}, f32[6,8,640]{2,1,0:T(8,128)}) custom-call(s32[1]{0:T(128)} %bitcast.odd_ref, s32[4]{0:T(128)} %valid_ref.1, f32[4,8,16,640]{3,2,1,0:T(8,128)} %maxima_ref.1, f32[3,16,640]{2,1,0:T(8,128)} %fields_ref.3, f32[3,16,640]{2,1,0:T(8,128)} %kappa_ref.3, s32[16,640]{1,0:T(8,128)} %mask_ref.3, ...), custom_call_target="tpu_custom_call" | custom-call | flops 99999997952 | bytes 1073741824 | tf_op jit(solution)/shard_map/likelihood/pallas_call | solution.py:184
  8.5 2.5 %all-to-all-done.1 = f32[8,1,128]{2,1,0:T(1,128)S(1)} async-done(((f32[8,1,128]{2,1,0:T(1,128)}), f32[8,1,128]{2,1,0:T(1,128)S(1)}, u32[]{:S(2)}, u32[]{:S(2)}) %all-to-all-start.1) | async-done | bytes 4128 | tf_op jit(solution)/shard_map/all_to_all | solution.py:177
  11.0 8.0 %all-to-all-start = ((f32[8,32,128]{2,1,0:T(8,128)}), f32[8,32,128]{2,1,0:T(8,128)S(1)}, u32[]{:S(2)}, u32[]{:S(2)}) async-start(f32[8,32,128]{2,1,0:T(8,128)} %bitcast.13), calls=%async_computation | async-start | bytes 262144 | tf_op jit(solution)/shard_map/all_to_all | solution.py:195
  19.0 10.5 %collective-permute-start = (f32[8,128]{1,0:T(8,128)S(1)}, f32[8,128]{1,0:T(8,128)S(1)}, u32[]{:S(2)}, u32[]{:S(2)}) collective-permute-start(f32[8,128]{1,0:T(8,128)S(1)} %bitcast.15), channel_id=1, source_target_pairs={{256,0},{321,1},{386,2},{451,3},{4,4},{69,5},{134,6},{199,7},{264,... | collective-permute-start | bytes 12296 | tf_op jit(solution)/shard_map/ppermute | solution.py:205
  29.4 1.9 %collective-permute-start.1 = (f32[6,8,640]{2,1,0:T(8,128)}, f32[6,8,640]{2,1,0:T(8,128)S(1)}, u32[]{:S(2)}, u32[]{:S(2)}) collective-permute-start(f32[6,8,640]{2,1,0:T(8,128)} %get-tuple-element.9), channel_id=1, source_target_pairs={{0,8},{8,0},{16,24},{24,16},{32,40},{40,32},{48,56},{56,48},{64,72... | collective-permute-start | bytes 368648 | tf_op jit(solution)/shard_map/ppermute | solution.py:215
  31.4 2.6 %collective-permute-start.2 = (f32[6,8,640]{2,1,0:T(8,128)}, f32[6,8,640]{2,1,0:T(8,128)S(1)}, u32[]{:S(2)}, u32[]{:S(2)}) collective-permute-start(f32[6,8,640]{2,1,0:T(8,128)} %get-tuple-element.10), channel_id=1, source_target_pairs={{0,504},{8,16},{16,8},{24,32},{32,24},{40,48},{48,40},{56,64},{64,... | collective-permute-start | bytes 368648 | tf_op jit(solution)/shard_map/ppermute | solution.py:217
  34.0 0.0 collective-permute-done.cells_ref
  34.0 0.0 all-to-all-done
  34.0 0.0 copy-start
  34.1 0.0 copy-start.1
  34.1 0.0 copy-start.2
  34.1 0.0 copy-start.3
  34.1 0.7 %middle.1 = f32[256,128]{1,0:T(8,128)} custom-call(f32[256,128]{1,0:T(8,128)S(1)} %bitcast.11, f32[8,128]{1,0:T(8,128)S(1)} %collective-permute-done.cells_ref), custom_call_target="tpu_custom_call" | custom-call | flops 99999997952 | bytes 1073741824 | tf_op jit(solution)/shard_map/middle/pallas_call | solution.py:206
  34.8 6.8 %all-to-all-start.2 = ((f32[8,32,128]{2,1,0:T(8,128)}), f32[8,32,128]{2,1,0:T(8,128)S(1)}, u32[]{:S(2)}, u32[]{:S(2)}) async-start(f32[8,32,128]{2,1,0:T(8,128)} %bitcast.6), calls=%async_computation.2 | async-start | bytes 262144 | tf_op jit(solution)/shard_map/all_to_all | solution.py:195
  41.6 0.0 collective-permute-done.1.inner_ref
  41.6 0.0 collective-permute-done.2.outer_ref
  41.6 0.0 copy-done
  41.6 0.0 copy-done.1
  41.6 0.0 copy-done.2
  41.7 2.4 %prior.1.refs_1_ = f32[3,16,640]{2,1,0:T(8,128)S(1)} custom-call(s32[1]{0:T(128)} %bitcast.odd_ref, f32[2,3]{1,0:T(2,128)S(1)} %bitcast.12, f32[3]{0:T(128)S(1)} %copy-done.3, f32[3,16,640]{2,1,0:T(8,128)S(1)} %copy-done, f32[3,16,640]{2,1,0:T(8,128)S(1)} %copy-done.1, f32[6,8,640]{2,1,0:T(8,128)S(1)} %collective-permute-done.1.inner_ref, ...), custom_call_target="tpu_custom_call" | custom-call | flops 99999997952 | bytes 1073741824 | tf_op jit(solution)/shard_map/prior/pallas_call | solution.py:220
  44.1 5.1 %all-to-all-done.2 = f32[8,32,128]{2,1,0:T(8,128)S(1)} async-done(((f32[8,32,128]{2,1,0:T(8,128)}), f32[8,32,128]{2,1,0:T(8,128)S(1)}, u32[]{:S(2)}, u32[]{:S(2)}) %all-to-all-start.2) | async-done | bytes 131104 | tf_op jit(solution)/shard_map/all_to_all | solution.py:195
  49.2 0.8 %final.1 = f32[3,16,640]{2,1,0:T(8,128)} custom-call(f32[256,128]{1,0:T(8,128)S(1)} %bitcast.10, f32[3,16,640]{2,1,0:T(8,128)S(1)} %prior.1.refs_1_), custom_call_target="tpu_custom_call" | custom-call | flops 61440 | bytes 368640 | tf_op jit(solution)/shard_map/final/pallas_call | solution.py:233
  (1 shorter events, 0.0 us)
Async XLA Ops:
  1.4 9.6 %all-to-all-start.1 = ((f32[8,1,128]{2,1,0:T(1,128)}), f32[8,1,128]{2,1,0:T(1,128)S(1)}, u32[]{:S(2)}, u32[]{:S(2)}) async-start(f32[8,1,128]{2,1,0:T(1,128)} %bitcast.14), calls=%async_computation.1 | async-start | bytes 8192 | tf_op jit(solution)/shard_map/all_to_all | solution.py:177
  11.0 23.1 %all-to-all-start = ((f32[8,32,128]{2,1,0:T(8,128)}), f32[8,32,128]{2,1,0:T(8,128)S(1)}, u32[]{:S(2)}, u32[]{:S(2)}) async-start(f32[8,32,128]{2,1,0:T(8,128)} %bitcast.13), calls=%async_computation | async-start | bytes 262144 | tf_op jit(solution)/shard_map/all_to_all | solution.py:195
  19.0 15.1 %collective-permute-start = (f32[8,128]{1,0:T(8,128)S(1)}, f32[8,128]{1,0:T(8,128)S(1)}, u32[]{:S(2)}, u32[]{:S(2)}) collective-permute-start(f32[8,128]{1,0:T(8,128)S(1)} %bitcast.15), channel_id=1, source_target_pairs={{256,0},{321,1},{386,2},{451,3},{4,4},{69,5},{134,6},{199,7},{264,... | collective-permute-start | bytes 12296 | tf_op jit(solution)/shard_map/ppermute | solution.py:205
  29.4 12.2 %collective-permute-start.1 = (f32[6,8,640]{2,1,0:T(8,128)}, f32[6,8,640]{2,1,0:T(8,128)S(1)}, u32[]{:S(2)}, u32[]{:S(2)}) collective-permute-start(f32[6,8,640]{2,1,0:T(8,128)} %get-tuple-element.9), channel_id=1, source_target_pairs={{0,8},{8,0},{16,24},{24,16},{32,40},{40,32},{48,56},{56,48},{64,72... | collective-permute-start | bytes 368648 | tf_op jit(solution)/shard_map/ppermute | solution.py:215
  31.4 10.2 %collective-permute-start.2 = (f32[6,8,640]{2,1,0:T(8,128)}, f32[6,8,640]{2,1,0:T(8,128)S(1)}, u32[]{:S(2)}, u32[]{:S(2)}) collective-permute-start(f32[6,8,640]{2,1,0:T(8,128)} %get-tuple-element.10), channel_id=1, source_target_pairs={{0,504},{8,16},{16,8},{24,32},{32,24},{40,48},{48,40},{56,64},{64,... | collective-permute-start | bytes 368648 | tf_op jit(solution)/shard_map/ppermute | solution.py:217
  34.0 7.6 %copy-start = (f32[3,16,640]{2,1,0:T(8,128)S(1)}, f32[3,16,640]{2,1,0:T(8,128)}, u32[]{:S(2)}) copy-start(f32[3,16,640]{2,1,0:T(8,128)} %fields_ref.3) | copy-start | bytes 368644
  34.1 7.6 %copy-start.1 = (f32[3,16,640]{2,1,0:T(8,128)S(1)}, f32[3,16,640]{2,1,0:T(8,128)}, u32[]{:S(2)}) copy-start(f32[3,16,640]{2,1,0:T(8,128)} %kappa_ref.3) | copy-start | bytes 368644
  34.1 7.6 %copy-start.2 = (f32[3,2]{0,1:T(2,128)S(1)}, f32[3,2]{0,1:T(2,128)}, u32[]{:S(2)}) copy-start(f32[3,2]{0,1:T(2,128)} %param.11) | copy-start | bytes 76
  34.1 7.6 %copy-start.3 = (f32[3]{0:T(128)S(1)}, f32[3]{0:T(128)}, u32[]{:S(2)}) copy-start(f32[3]{0:T(128)} %precision_ref.1) | copy-start | bytes 40
  34.8 14.5 %all-to-all-start.2 = ((f32[8,32,128]{2,1,0:T(8,128)}), f32[8,32,128]{2,1,0:T(8,128)S(1)}, u32[]{:S(2)}, u32[]{:S(2)}) async-start(f32[8,32,128]{2,1,0:T(8,128)} %bitcast.6), calls=%async_computation.2 | async-start | bytes 262144 | tf_op jit(solution)/shard_map/all_to_all | solution.py:195

commit v4 on v3

--- a/solution.py
+++ b/solution.py
@@ -11,6 +11,7 @@
 SUB = 8
 MIB = 1 << 20
 PIECE = 32
+PARTNER = (0, 1, 2, 5, 4, 6, 7, 3)
 CELL_ROW = 30
 YEAR_ROW = 31
 VMEM = pl.BlockSpec(memory_space=pltpu.VMEM)
@@ -165,7 +166,7 @@
     f32 = jnp.float32
     rows, columns = fields.shape[1:]
     spaces, groups = lax.axis_size("space"), lax.axis_size("years")
-    planes = [list(range(z, z + SUB)) for z in range(0, spaces, SUB)]
+    planes = [[z + (a + SUB // 2) % SUB for a in range(SUB)] for z in range(0, spaces, SUB)]
     cells = pl.pallas_call(
         cells_kernel,
         out_shape=jax.ShapeDtypeStruct((SUB, LANES), f32),
@@ -192,12 +193,15 @@
 
     def exchange(pieces):
         pieces = pieces.reshape(groups, PIECE, LANES)
-        pieces = lax.all_to_all(pieces, "years", 0, 0, tiled=True)
+        order = [(i + groups // 2) % groups for i in range(groups)]
+        pieces = lax.all_to_all(
+            pieces, "years", 0, 0, tiled=True, axis_index_groups=[order]
+        )
         return pieces.reshape(groups * PIECE, LANES)
 
     parts = exchange(packed)
     far = [
-        (((z ^ y ^ 4) * SUB + a) * groups + y, (z * SUB + a) * groups + y)
+        (((z ^ PARTNER[y]) * SUB + a) * groups + y, (z * SUB + a) * groups + y)
         for z in range(spaces // SUB)
         for a in range(SUB)
         for y in range(groups)

time: 50.5 us -> 48.2 us (0.954)
  the two profiles are of different devices: /device:TPU:8 before, /device:TPU:16 now
where the time goes in v4:
time: 48.2 us; the launch traced here: 47.7 us
  starting transfers between devices  36.7 us (76%)
  Pallas kernels  7.99 us (17%)
  waiting for transfers between devices  2.88 us (6%)
    all_to_all x2, starting transfers between devices, exchange(): lax.all_to_all(pieces, 'years', 0, 0, tiled=True, axis_index_groups=[order])  15.5 us
    ppermute x1, starting transfers between devices, local(): from_outer = lax.ppermute(outer, 'space', outer_pairs)  9.07 us
    all_to_all x1, starting transfers between devices, local(): lax.all_to_all(cells[:, None], 'space', 0, 0, tiled=True, axis_index_grou...  6.22 us
    ppermute x1, starting transfers between devices, local(): far_cells = lax.ppermute(plane_cells, ('space', 'years'), far)  4.04 us
    all_to_all x2, waiting for transfers between devices, exchange(): lax.all_to_all(pieces, 'years', 0, 0, tiled=True, axis_index_groups=[order])  2.87 us
    pallas_call x1, Pallas kernels, local(): pl.pallas_call(likelihood_kernel, out_shape=(packed_shape, halo_shape, ha...  2.74 us
    pallas_call x1, Pallas kernels, local(): pl.pallas_call(prior_kernel, out_shape=jax.ShapeDtypeStruct(fields.shape,...  2.42 us
    ppermute x1, starting transfers between devices, local(): lax.ppermute(inner, 'space', [(s, s ^ 1) for s in range(spaces)])  1.92 us
  transfers between devices with their start and end apart: 6, of which 1 were waited for; matrix products, arithmetic and copies ran while one was open for 0% of the time, Pallas kernels for 12%

profile of v4, /device:TPU:16, one launch (start us, length us, event | category | flops | bytes accessed | tf_op | source)
XLA Modules:
  0.0 47.7 jit_solution(1554915813296880174)
XLA Ops:
  0.0 1.4 %cells.1 = f32[8,128]{1,0:T(8,128)} custom-call(s32[16,640]{1,0:T(8,128)} %mask_ref.3, s32[16,640]{1,0:T(8,128)} %counts_ref.3), custom_call_target="tpu_custom_call" | custom-call | flops 20480 | bytes 81920 | tf_op jit(solution)/shard_map/cells/pallas_call | solution.py:170
  1.4 6.2 %all-to-all-start.1 = ((f32[8,1,128]{2,1,0:T(1,128)}), f32[8,1,128]{2,1,0:T(1,128)S(1)}, u32[]{:S(2)}, u32[]{:S(2)}) async-start(f32[8,1,128]{2,1,0:T(1,128)} %bitcast.14), calls=%async_computation.1 | async-start | bytes 8192 | tf_op jit(solution)/shard_map/all_to_all | solution.py:178
  7.6 2.7 %likelihood.1 = (f32[256,128]{1,0:T(8,128)}, f32[6,8,640]{2,1,0:T(8,128)}, f32[6,8,640]{2,1,0:T(8,128)}) custom-call(s32[1]{0:T(128)} %bitcast.odd_ref, s32[4]{0:T(128)} %valid_ref.1, f32[4,8,16,640]{3,2,1,0:T(8,128)} %maxima_ref.1, f32[3,16,640]{2,1,0:T(8,128)} %fields_ref.3, f32[3,16,640]{2,1,0:T(8,128)} %kappa_ref.3, s32[16,640]{1,0:T(8,128)} %mask_ref.3, ...), custom_call_target="tpu_custom_call" | custom-call | flops 99999997952 | bytes 1073741824 | tf_op jit(solution)/shard_map/likelihood/pallas_call | solution.py:185
  10.4 0.0 all-to-all-done.1
  10.4 9.1 %all-to-all-start = ((f32[8,32,128]{2,1,0:T(8,128)}), f32[8,32,128]{2,1,0:T(8,128)S(1)}, u32[]{:S(2)}, u32[]{:S(2)}) async-start(f32[8,32,128]{2,1,0:T(8,128)} %bitcast.13), calls=%async_computation | async-start | bytes 262144 | tf_op jit(solution)/shard_map/all_to_all | solution.py:197
  19.5 4.0 %collective-permute-start = (f32[8,128]{1,0:T(8,128)S(1)}, f32[8,128]{1,0:T(8,128)S(1)}, u32[]{:S(2)}, u32[]{:S(2)}) collective-permute-start(f32[8,128]{1,0:T(8,128)S(1)} %bitcast.15), channel_id=1, source_target_pairs={{0,0},{65,1},{130,2},{323,3},{260,4},{389,5},{454,6},{199,7},{8,8}... | collective-permute-start | bytes 12296 | tf_op jit(solution)/shard_map/ppermute | solution.py:209
  23.6 1.9 %collective-permute-start.1 = (f32[6,8,640]{2,1,0:T(8,128)}, f32[6,8,640]{2,1,0:T(8,128)S(1)}, u32[]{:S(2)}, u32[]{:S(2)}) collective-permute-start(f32[6,8,640]{2,1,0:T(8,128)} %get-tuple-element.9), channel_id=1, source_target_pairs={{0,8},{8,0},{16,24},{24,16},{32,40},{40,32},{48,56},{56,48},{64,72... | collective-permute-start | bytes 368648 | tf_op jit(solution)/shard_map/ppermute | solution.py:219
  25.5 9.1 %collective-permute-start.2 = (f32[6,8,640]{2,1,0:T(8,128)}, f32[6,8,640]{2,1,0:T(8,128)S(1)}, u32[]{:S(2)}, u32[]{:S(2)}) collective-permute-start(f32[6,8,640]{2,1,0:T(8,128)} %get-tuple-element.10), channel_id=1, source_target_pairs={{0,504},{8,16},{16,8},{24,32},{32,24},{40,48},{48,40},{56,64},{64,... | collective-permute-start | bytes 368648 | tf_op jit(solution)/shard_map/ppermute | solution.py:221
  34.6 0.0 collective-permute-done.cells_ref
  34.6 0.0 all-to-all-done
  34.6 0.0 copy-start
  34.6 0.0 copy-start.1
  34.6 0.0 copy-start.2
  34.6 0.0 copy-start.3
  34.6 0.7 %middle.1 = f32[256,128]{1,0:T(8,128)} custom-call(f32[256,128]{1,0:T(8,128)S(1)} %bitcast.11, f32[8,128]{1,0:T(8,128)S(1)} %collective-permute-done.cells_ref), custom_call_target="tpu_custom_call" | custom-call | flops 99999997952 | bytes 1073741824 | tf_op jit(solution)/shard_map/middle/pallas_call | solution.py:210
  35.3 6.3 %all-to-all-start.2 = ((f32[8,32,128]{2,1,0:T(8,128)}), f32[8,32,128]{2,1,0:T(8,128)S(1)}, u32[]{:S(2)}, u32[]{:S(2)}) async-start(f32[8,32,128]{2,1,0:T(8,128)} %bitcast.6), calls=%async_computation.2 | async-start | bytes 262144 | tf_op jit(solution)/shard_map/all_to_all | solution.py:197
  41.6 0.0 collective-permute-done.1.inner_ref
  41.6 0.0 collective-permute-done.2.outer_ref
  41.6 0.0 copy-done
  41.6 0.0 copy-done.1
  41.6 0.0 copy-done.2
  41.7 2.4 %prior.1.refs_1_ = f32[3,16,640]{2,1,0:T(8,128)S(1)} custom-call(s32[1]{0:T(128)} %bitcast.odd_ref, f32[2,3]{1,0:T(2,128)S(1)} %bitcast.12, f32[3]{0:T(128)S(1)} %copy-done.3, f32[3,16,640]{2,1,0:T(8,128)S(1)} %copy-done, f32[3,16,640]{2,1,0:T(8,128)S(1)} %copy-done.1, f32[6,8,640]{2,1,0:T(8,128)S(1)} %collective-permute-done.1.inner_ref, ...), custom_call_target="tpu_custom_call" | custom-call | flops 99999997952 | bytes 1073741824 | tf_op jit(solution)/shard_map/prior/pallas_call | solution.py:224
  44.1 2.9 %all-to-all-done.2 = f32[8,32,128]{2,1,0:T(8,128)S(1)} async-done(((f32[8,32,128]{2,1,0:T(8,128)}), f32[8,32,128]{2,1,0:T(8,128)S(1)}, u32[]{:S(2)}, u32[]{:S(2)}) %all-to-all-start.2) | async-done | bytes 131104 | tf_op jit(solution)/shard_map/all_to_all | solution.py:197
  47.0 0.8 %final.1 = f32[3,16,640]{2,1,0:T(8,128)} custom-call(f32[256,128]{1,0:T(8,128)S(1)} %bitcast.10, f32[3,16,640]{2,1,0:T(8,128)S(1)} %prior.1.refs_1_), custom_call_target="tpu_custom_call" | custom-call | flops 61440 | bytes 368640 | tf_op jit(solution)/shard_map/final/pallas_call | solution.py:237
  (1 shorter events, 0.0 us)
Async XLA Ops:
  1.4 9.0 %all-to-all-start.1 = ((f32[8,1,128]{2,1,0:T(1,128)}), f32[8,1,128]{2,1,0:T(1,128)S(1)}, u32[]{:S(2)}, u32[]{:S(2)}) async-start(f32[8,1,128]{2,1,0:T(1,128)} %bitcast.14), calls=%async_computation.1 | async-start | bytes 8192 | tf_op jit(solution)/shard_map/all_to_all | solution.py:178
  10.4 24.2 %all-to-all-start = ((f32[8,32,128]{2,1,0:T(8,128)}), f32[8,32,128]{2,1,0:T(8,128)S(1)}, u32[]{:S(2)}, u32[]{:S(2)}) async-start(f32[8,32,128]{2,1,0:T(8,128)} %bitcast.13), calls=%async_computation | async-start | bytes 262144 | tf_op jit(solution)/shard_map/all_to_all | solution.py:197
  19.5 15.1 %collective-permute-start = (f32[8,128]{1,0:T(8,128)S(1)}, f32[8,128]{1,0:T(8,128)S(1)}, u32[]{:S(2)}, u32[]{:S(2)}) collective-permute-start(f32[8,128]{1,0:T(8,128)S(1)} %bitcast.15), channel_id=1, source_target_pairs={{0,0},{65,1},{130,2},{323,3},{260,4},{389,5},{454,6},{199,7},{8,8}... | collective-permute-start | bytes 12296 | tf_op jit(solution)/shard_map/ppermute | solution.py:209
  23.6 18.1 %collective-permute-start.1 = (f32[6,8,640]{2,1,0:T(8,128)}, f32[6,8,640]{2,1,0:T(8,128)S(1)}, u32[]{:S(2)}, u32[]{:S(2)}) collective-permute-start(f32[6,8,640]{2,1,0:T(8,128)} %get-tuple-element.9), channel_id=1, source_target_pairs={{0,8},{8,0},{16,24},{24,16},{32,40},{40,32},{48,56},{56,48},{64,72... | collective-permute-start | bytes 368648 | tf_op jit(solution)/shard_map/ppermute | solution.py:219
  25.5 16.1 %collective-permute-start.2 = (f32[6,8,640]{2,1,0:T(8,128)}, f32[6,8,640]{2,1,0:T(8,128)S(1)}, u32[]{:S(2)}, u32[]{:S(2)}) collective-permute-start(f32[6,8,640]{2,1,0:T(8,128)} %get-tuple-element.10), channel_id=1, source_target_pairs={{0,504},{8,16},{16,8},{24,32},{32,24},{40,48},{48,40},{56,64},{64,... | collective-permute-start | bytes 368648 | tf_op jit(solution)/shard_map/ppermute | solution.py:221
  34.6 7.0 %copy-start = (f32[3,16,640]{2,1,0:T(8,128)S(1)}, f32[3,16,640]{2,1,0:T(8,128)}, u32[]{:S(2)}) copy-start(f32[3,16,640]{2,1,0:T(8,128)} %fields_ref.3) | copy-start | bytes 368644
  34.6 7.0 %copy-start.1 = (f32[3,16,640]{2,1,0:T(8,128)S(1)}, f32[3,16,640]{2,1,0:T(8,128)}, u32[]{:S(2)}) copy-start(f32[3,16,640]{2,1,0:T(8,128)} %kappa_ref.3) | copy-start | bytes 368644
  34.6 7.0 %copy-start.2 = (f32[3,2]{0,1:T(2,128)S(1)}, f32[3,2]{0,1:T(2,128)}, u32[]{:S(2)}) copy-start(f32[3,2]{0,1:T(2,128)} %param.11) | copy-start | bytes 76
  34.6 7.0 %copy-start.3 = (f32[3]{0:T(128)S(1)}, f32[3]{0:T(128)}, u32[]{:S(2)}) copy-start(f32[3]{0:T(128)} %precision_ref.1) | copy-start | bytes 40
  35.3 11.7 %all-to-all-start.2 = ((f32[8,32,128]{2,1,0:T(8,128)}), f32[8,32,128]{2,1,0:T(8,128)S(1)}, u32[]{:S(2)}, u32[]{:S(2)}) async-start(f32[8,32,128]{2,1,0:T(8,128)} %bitcast.6), calls=%async_computation.2 | async-start | bytes 262144 | tf_op jit(solution)/shard_map/all_to_all | solution.py:197

commit v5 on v4

--- a/solution.py
+++ b/solution.py
@@ -1,3 +1,5 @@
+import functools
+
 import jax
 import jax.numpy as jnp
 from jax import lax
@@ -11,6 +13,7 @@
 SUB = 8
 MIB = 1 << 20
 PIECE = 32
+EARLY = 16
 PARTNER = (0, 1, 2, 5, 4, 6, 7, 3)
 CELL_ROW = 30
 YEAR_ROW = 31
@@ -35,9 +38,13 @@
     cells_ref[...] = jnp.broadcast_to(total, cells_ref.shape)
 
 
+def rounds(here, last):
+    return here < 2, (here == 0) | (here == last), here >= last - 1
+
+
 def likelihood_kernel(
-    odd_ref, valid_ref, maxima_ref, fields_ref, kappa_ref, mask_ref, counts_ref,
-    packed_ref, inner_ref, outer_ref,
+    here_ref, valid_ref, maxima_ref, fields_ref, kappa_ref, mask_ref, counts_ref,
+    packed_ref, early_ref, first_ref, second_ref, *, end,
 ):
     years, orders, rows, columns = maxima_ref.shape
     row_tiles, lane_tiles = rows // SUB, columns // LANES
@@ -100,30 +107,44 @@
         packed_ref[place(q), :] = tile
     packed_ref[pl.ds(CELL_ROW, SUB, PIECE), :] = jnp.zeros((SUB, LANES), jnp.float32)
     packed_ref[pl.ds(YEAR_ROW, SUB, PIECE), :] = jnp.full((SUB, LANES), valid_sum, jnp.float32)
-    inner_row = pl.multiple_of((1 - odd_ref[0]) * (rows - HALO), HALO)
-    outer_row = pl.multiple_of(odd_ref[0] * (rows - HALO), HALO)
-    inner_ref[0:3] = fields_ref[:, pl.ds(inner_row, HALO)]
-    inner_ref[3:6] = kappa_ref[:, pl.ds(inner_row, HALO)]
-    outer_ref[0:3] = fields_ref[:, pl.ds(outer_row, HALO)]
-    outer_ref[3:6] = kappa_ref[:, pl.ds(outer_row, HALO)]
+    here = here_ref[0]
+    odd = lax.rem(here, 2)
+    early_swapped, first_swapped, second_swapped = rounds(here, end)
+    halves = (
+        jnp.where(early_swapped, 1 - odd, odd),
+        jnp.where(first_swapped, odd, 1 - odd),
+        jnp.where(second_swapped, 1 - odd, odd),
+    )
+    for pack_ref, half in zip((early_ref, first_ref, second_ref), halves):
+        at = pl.ds(pl.multiple_of(half * (rows - HALO), HALO), HALO)
+        pack_ref[0:3] = fields_ref[:, at]
+        pack_ref[3:6] = kappa_ref[:, at]
 
 
 def prior_kernel(
-    odd_ref, aniso_ref, precision_ref, fields_ref, kappa_ref, inner_ref, outer_ref, out_ref
+    here_ref, aniso_ref, precision_ref, fields_ref, kappa_ref,
+    early_ref, first_ref, second_ref, out_ref, *, last,
 ):
     rows, columns = fields_ref.shape[1:]
     extent = rows + 2 * HALO
     lane = lax.broadcasted_iota(jnp.int32, (extent, columns), 1)
-    odd = odd_ref[0] == 1
-
-    def between(inner, rows_here, outer):
+    here = here_ref[0]
+    odd = lax.rem(here, 2) == 1
+    early_swapped, first_swapped, second_swapped = rounds(here, last)
+
+    def between(rows_here, i):
+        early, first, second = early_ref[i], first_ref[i], second_ref[i]
+        inner = jnp.where(early_swapped, early, 0.0) + jnp.where(first_swapped, 0.0, first)
+        inner = inner + jnp.where(second_swapped, second, 0.0)
+        outer = jnp.where(early_swapped, 0.0, early) + jnp.where(first_swapped, first, 0.0)
+        outer = outer + jnp.where(second_swapped, 0.0, second)
         low, high = jnp.where(odd, inner, outer), jnp.where(odd, outer, inner)
         return jnp.concatenate([low, rows_here, high], axis=0)
 
     for f in range(3):
         zonal, meridional = aniso_ref[0, f], aniso_ref[1, f]
-        values = between(inner_ref[f], fields_ref[f], outer_ref[f])
-        centre = between(inner_ref[3 + f], kappa_ref[f], outer_ref[3 + f])
+        values = between(fields_ref[f], f)
+        centre = between(kappa_ref[f], 3 + f)
         centre = centre + (2.0 * zonal + 2.0 * meridional)
         for _ in range(SWEEPS):
             east_west = pltpu.roll(values, 1, 0) + pltpu.roll(values, extent - 1, 0)
@@ -179,17 +200,17 @@
         cells[:, None], "space", 0, 0, tiled=True, axis_index_groups=planes
     )[:, 0]
 
-    odd = (lax.axis_index("space") % 2).astype(jnp.int32).reshape(1)
+    here = lax.axis_index("space").astype(jnp.int32).reshape(1)
     halo_shape = jax.ShapeDtypeStruct((6, HALO, columns), f32)
     packed_shape = jax.ShapeDtypeStruct((groups * PIECE, LANES), f32)
-    packed, inner, outer = pl.pallas_call(
-        likelihood_kernel,
-        out_shape=(packed_shape, halo_shape, halo_shape),
+    packed, early, first, second = pl.pallas_call(
+        functools.partial(likelihood_kernel, end=spaces - 1),
+        out_shape=(packed_shape,) + (halo_shape,) * 3,
         in_specs=[SMEM] * 2 + [VMEM] * 5,
-        out_specs=(VMEM,) * 3,
+        out_specs=(VMEM,) * 4,
         cost_estimate=pl.CostEstimate(flops=10**11, bytes_accessed=1024 * MIB, transcendentals=0),
         name="likelihood",
-    )(odd, year_valid, maxima, fields, kappa_sq, ocean_mask, counts)
+    )(here, year_valid, maxima, fields, kappa_sq, ocean_mask, counts)
 
     def exchange(pieces):
         pieces = pieces.reshape(groups, PIECE, LANES)
@@ -207,6 +228,16 @@
         for y in range(groups)
     ]
     far_cells = lax.ppermute(plane_cells, ("space", "years"), far)
+    inner_pairs = [(s, s ^ 1) for s in range(spaces)]
+    outer_pairs = [(s, (s + (1 if s % 2 else -1)) % spaces) for s in range(spaces)]
+    last = spaces - 1
+    early_pairs = [(0, 1), (1, 0), (last - 2, last - 1), (last - 1, last - 2)]
+    early_pairs += [pair for pair in outer_pairs if 2 < min(pair) and max(pair) < EARLY]
+    first_pairs = [pair for pair in inner_pairs if 1 < min(pair) and max(pair) < last - 1]
+    first_pairs += [(0, last), (last, 0)]
+    second_pairs = [pair for pair in inner_pairs + outer_pairs if pair not in early_pairs + first_pairs]
+    from_early = lax.ppermute(early, "space", early_pairs)
+    parts, far_cells, from_early = lax.optimization_barrier((parts, far_cells, from_early))
     spread = pl.pallas_call(
         middle_kernel,
         out_shape=packed_shape,
@@ -216,22 +247,21 @@
         compiler_params=pltpu.CompilerParams(vmem_limit_bytes=3 * MIB),
         name="middle",
     )(parts, far_cells)
-    from_inner = lax.ppermute(inner, "space", [(s, s ^ 1) for s in range(spaces)])
-    outer_pairs = [(s, (s + (1 if s % 2 else -1)) % spaces) for s in range(spaces)]
-    from_outer = lax.ppermute(outer, "space", outer_pairs)
+    from_first = lax.ppermute(first, "space", first_pairs)
+    from_second = lax.ppermute(lax.optimization_barrier(second), "space", second_pairs)
     whole = exchange(spread)
 
     prior = pl.pallas_call(
-        prior_kernel,
+        functools.partial(prior_kernel, last=last),
         out_shape=jax.ShapeDtypeStruct(fields.shape, f32),
-        in_specs=[SMEM] * 3 + [VMEM] * 4,
+        in_specs=[SMEM] * 3 + [VMEM] * 5,
         out_specs=VMEM,
         cost_estimate=pl.CostEstimate(
             flops=10**11, bytes_accessed=1024 * MIB, transcendentals=0
         ),
         compiler_params=pltpu.CompilerParams(vmem_limit_bytes=6 * MIB),
         name="prior",
-    )(odd, anisotropy.T, precision, fields, kappa_sq, from_inner, from_outer)
+    )(here, anisotropy.T, precision, fields, kappa_sq, from_early, from_first, from_second)
 
     grid_cells = float(rows * spaces * columns)
     return pl.pallas_call(

time: 48.2 us -> 46.4 us (0.963)
  the two profiles are of different devices: /device:TPU:16 before, /device:TPU:8 now
where the time goes in v5:
time: 46.4 us; the launch traced here: 45.9 us
  starting transfers between devices  35.8 us (77%)
  Pallas kernels  7.99 us (17%)
  waiting for transfers between devices  1.96 us (4%)
    all_to_all x2, starting transfers between devices, exchange(): lax.all_to_all(pieces, 'years', 0, 0, tiled=True, axis_index_groups=[order])  16.5 us
    all_to_all x1, starting transfers between devices, local(): lax.all_to_all(cells[:, None], 'space', 0, 0, tiled=True, axis_index_grou...  6.19 us
    ppermute x1, starting transfers between devices, local(): from_first = lax.ppermute(first, 'space', first_pairs)  6.17 us
    ppermute x1, starting transfers between devices, local(): far_cells = lax.ppermute(plane_cells, ('space', 'years'), far)  4.39 us
    pallas_call x1, Pallas kernels, local(): pl.pallas_call(functools.partial(likelihood_kernel, end=spaces - 1), out_...  2.77 us
    pallas_call x1, Pallas kernels, local(): pl.pallas_call(functools.partial(prior_kernel, last=last), out_shape=jax....  2.38 us
    all_to_all x2, waiting for transfers between devices, exchange(): lax.all_to_all(pieces, 'years', 0, 0, tiled=True, axis_index_groups=[order])  1.95 us
    ppermute x1, starting transfers between devices, local(): from_early = lax.ppermute(early, 'space', early_pairs)  1.91 us
  transfers between devices with their start and end apart: 7, of which 1 were waited for; matrix products, arithmetic and copies ran while one was open for 0% of the time, Pallas kernels for 13%

profile of v5, /device:TPU:8, one launch (start us, length us, event | category | flops | bytes accessed | tf_op | source)
XLA Modules:
  0.0 45.9 jit_solution(7439421487915114756)
XLA Ops:
  0.0 1.4 %cells.1 = f32[8,128]{1,0:T(8,128)} custom-call(s32[16,640]{1,0:T(8,128)} %mask_ref.3, s32[16,640]{1,0:T(8,128)} %counts_ref.3), custom_call_target="tpu_custom_call" | custom-call | flops 20480 | bytes 81920 | tf_op jit(solution)/shard_map/cells/pallas_call | solution.py:191
  1.4 6.2 %all-to-all-start.1 = ((f32[8,1,128]{2,1,0:T(1,128)}), f32[8,1,128]{2,1,0:T(1,128)S(1)}, u32[]{:S(2)}, u32[]{:S(2)}) async-start(f32[8,1,128]{2,1,0:T(1,128)} %bitcast.14), calls=%async_computation.1 | async-start | bytes 8192 | tf_op jit(solution)/shard_map/all_to_all | solution.py:199
  7.6 2.8 %likelihood.1 = (f32[256,128]{1,0:T(8,128)}, f32[6,8,640]{2,1,0:T(8,128)}, f32[6,8,640]{2,1,0:T(8,128)}, f32[6,8,640]{2,1,0:T(8,128)}) custom-call(s32[1]{0:T(128)} %bitcast.here_ref, s32[4]{0:T(128)} %valid_ref.1, f32[4,8,16,640]{3,2,1,0:T(8,128)} %maxima_ref.1, f32[3,16,640]{2,1,0:T(8,128)} %fields_ref.3, f32[3,16,640]{2,1,0:T(8,128)} %kappa_ref.3, ...), custom_call_target="tpu_custom_call" | custom-call | flops 99999997952 | bytes 1073741824 | tf_op jit(solution)/shard_map/likelihood/pallas_call | solution.py:206
  10.4 0.0 all-to-all-done.1
  10.4 10.2 %all-to-all-start = ((f32[8,32,128]{2,1,0:T(8,128)}), f32[8,32,128]{2,1,0:T(8,128)S(1)}, u32[]{:S(2)}, u32[]{:S(2)}) async-start(f32[8,32,128]{2,1,0:T(8,128)} %bitcast.13), calls=%async_computation | async-start | bytes 262144 | tf_op jit(solution)/shard_map/all_to_all | solution.py:218
  20.6 1.9 %collective-permute-start.1 = (f32[6,8,640]{2,1,0:T(8,128)}, f32[6,8,640]{2,1,0:T(8,128)S(1)}, u32[]{:S(2)}, u32[]{:S(2)}) collective-permute-start(f32[6,8,640]{2,1,0:T(8,128)} %get-tuple-element.13), channel_id=1, source_target_pairs={{0,8},{8,0},{488,496},{496,488},{24,32},{32,24},{40,48},{48,40},{5... | collective-permute-start | bytes 368648 | tf_op jit(solution)/shard_map/ppermute | solution.py:239
  22.5 4.4 %collective-permute-start = (f32[8,128]{1,0:T(8,128)S(1)}, f32[8,128]{1,0:T(8,128)S(1)}, u32[]{:S(2)}, u32[]{:S(2)}) collective-permute-start(f32[8,128]{1,0:T(8,128)S(1)} %bitcast.15), channel_id=1, source_target_pairs={{0,0},{65,1},{130,2},{323,3},{260,4},{389,5},{454,6},{199,7},{8,8}... | collective-permute-start | bytes 12296 | tf_op jit(solution)/shard_map/ppermute | solution.py:230
  26.9 6.2 %collective-permute-start.2 = (f32[6,8,640]{2,1,0:T(8,128)}, f32[6,8,640]{2,1,0:T(8,128)S(1)}, u32[]{:S(2)}, u32[]{:S(2)}) collective-permute-start(f32[6,8,640]{2,1,0:T(8,128)} %get-tuple-element.17), channel_id=1, source_target_pairs={{16,24},{24,16},{32,40},{40,32},{48,56},{56,48},{64,72},{72,64},{8... | collective-permute-start | bytes 368648 | tf_op jit(solution)/shard_map/ppermute | solution.py:250
  33.1 0.7 %collective-permute-start.3 = (f32[6,8,640]{2,1,0:T(8,128)}, f32[6,8,640]{2,1,0:T(8,128)S(1)}, u32[]{:S(2)}, u32[]{:S(2)}) collective-permute-start(f32[6,8,640]{2,1,0:T(8,128)} %get-tuple-element.18), channel_id=1, source_target_pairs={{496,504},{504,496},{8,16},{16,8},{120,128},{128,120},{136,144},{1... | collective-permute-start | bytes 368648 | tf_op jit(solution)/shard_map/ppermute | solution.py:251
  33.7 0.0 collective-permute-done.cells_ref
  33.7 0.0 collective-permute-done.1.early_ref
  33.8 0.0 all-to-all-done
  33.8 0.0 copy-start
  33.8 0.0 copy-start.1
  33.8 0.0 copy-start.2
  33.8 0.0 copy-start.3
  33.8 0.7 %middle.1 = f32[256,128]{1,0:T(8,128)} custom-call(f32[256,128]{1,0:T(8,128)S(1)} %bitcast.11, f32[8,128]{1,0:T(8,128)S(1)} %collective-permute-done.cells_ref), custom_call_target="tpu_custom_call" | custom-call | flops 99999997952 | bytes 1073741824 | tf_op jit(solution)/shard_map/middle/pallas_call | solution.py:241
  34.5 6.3 %all-to-all-start.2 = ((f32[8,32,128]{2,1,0:T(8,128)}), f32[8,32,128]{2,1,0:T(8,128)S(1)}, u32[]{:S(2)}, u32[]{:S(2)}) async-start(f32[8,32,128]{2,1,0:T(8,128)} %bitcast.6), calls=%async_computation.2 | async-start | bytes 262144 | tf_op jit(solution)/shard_map/all_to_all | solution.py:218
  40.8 0.0 collective-permute-done.2.first_ref
  40.8 0.0 collective-permute-done.3.second_ref
  40.8 0.0 copy-done
  40.8 2.4 %prior.1.refs_1_ = f32[3,16,640]{2,1,0:T(8,128)S(1)} custom-call(s32[1]{0:T(128)} %bitcast.here_ref, f32[2,3]{1,0:T(2,128)S(1)} %bitcast.12, f32[3]{0:T(128)S(1)} %copy-done.3, f32[3,16,640]{2,1,0:T(8,128)S(1)} %copy-done, f32[3,16,640]{2,1,0:T(8,128)S(1)} %copy-done.1, f32[6,8,640]{2,1,0:T(8,128)S(1)} %collective-permute-done.1.early_ref, ...), custom_call_target="tpu_custom_call" | custom-call | flops 99999997952 | bytes 1073741824 | tf_op jit(solution)/shard_map/prior/pallas_call | solution.py:254
  43.2 1.9 %all-to-all-done.2 = f32[8,32,128]{2,1,0:T(8,128)S(1)} async-done(((f32[8,32,128]{2,1,0:T(8,128)}), f32[8,32,128]{2,1,0:T(8,128)S(1)}, u32[]{:S(2)}, u32[]{:S(2)}) %all-to-all-start.2) | async-done | bytes 131104 | tf_op jit(solution)/shard_map/all_to_all | solution.py:218
  45.2 0.8 %final.1 = f32[3,16,640]{2,1,0:T(8,128)} custom-call(f32[256,128]{1,0:T(8,128)S(1)} %bitcast.10, f32[3,16,640]{2,1,0:T(8,128)S(1)} %prior.1.refs_1_), custom_call_target="tpu_custom_call" | custom-call | flops 61440 | bytes 368640 | tf_op jit(solution)/shard_map/final/pallas_call | solution.py:267
  (3 shorter events, 0.0 us)
Async XLA Ops:
  1.4 9.0 %all-to-all-start.1 = ((f32[8,1,128]{2,1,0:T(1,128)}), f32[8,1,128]{2,1,0:T(1,128)S(1)}, u32[]{:S(2)}, u32[]{:S(2)}) async-start(f32[8,1,128]{2,1,0:T(1,128)} %bitcast.14), calls=%async_computation.1 | async-start | bytes 8192 | tf_op jit(solution)/shard_map/all_to_all | solution.py:199
  10.4 23.4 %all-to-all-start = ((f32[8,32,128]{2,1,0:T(8,128)}), f32[8,32,128]{2,1,0:T(8,128)S(1)}, u32[]{:S(2)}, u32[]{:S(2)}) async-start(f32[8,32,128]{2,1,0:T(8,128)} %bitcast.13), calls=%async_computation | async-start | bytes 262144 | tf_op jit(solution)/shard_map/all_to_all | solution.py:218
  20.6 13.2 %collective-permute-start.1 = (f32[6,8,640]{2,1,0:T(8,128)}, f32[6,8,640]{2,1,0:T(8,128)S(1)}, u32[]{:S(2)}, u32[]{:S(2)}) collective-permute-start(f32[6,8,640]{2,1,0:T(8,128)} %get-tuple-element.13), channel_id=1, source_target_pairs={{0,8},{8,0},{488,496},{496,488},{24,32},{32,24},{40,48},{48,40},{5... | collective-permute-start | bytes 368648 | tf_op jit(solution)/shard_map/ppermute | solution.py:239
  22.5 11.3 %collective-permute-start = (f32[8,128]{1,0:T(8,128)S(1)}, f32[8,128]{1,0:T(8,128)S(1)}, u32[]{:S(2)}, u32[]{:S(2)}) collective-permute-start(f32[8,128]{1,0:T(8,128)S(1)} %bitcast.15), channel_id=1, source_target_pairs={{0,0},{65,1},{130,2},{323,3},{260,4},{389,5},{454,6},{199,7},{8,8}... | collective-permute-start | bytes 12296 | tf_op jit(solution)/shard_map/ppermute | solution.py:230
  26.9 13.9 %collective-permute-start.2 = (f32[6,8,640]{2,1,0:T(8,128)}, f32[6,8,640]{2,1,0:T(8,128)S(1)}, u32[]{:S(2)}, u32[]{:S(2)}) collective-permute-start(f32[6,8,640]{2,1,0:T(8,128)} %get-tuple-element.17), channel_id=1, source_target_pairs={{16,24},{24,16},{32,40},{40,32},{48,56},{56,48},{64,72},{72,64},{8... | collective-permute-start | bytes 368648 | tf_op jit(solution)/shard_map/ppermute | solution.py:250
  33.1 7.7 %collective-permute-start.3 = (f32[6,8,640]{2,1,0:T(8,128)}, f32[6,8,640]{2,1,0:T(8,128)S(1)}, u32[]{:S(2)}, u32[]{:S(2)}) collective-permute-start(f32[6,8,640]{2,1,0:T(8,128)} %get-tuple-element.18), channel_id=1, source_target_pairs={{496,504},{504,496},{8,16},{16,8},{120,128},{128,120},{136,144},{1... | collective-permute-start | bytes 368648 | tf_op jit(solution)/shard_map/ppermute | solution.py:251
  33.8 7.0 %copy-start = (f32[3,16,640]{2,1,0:T(8,128)S(1)}, f32[3,16,640]{2,1,0:T(8,128)}, u32[]{:S(2)}) copy-start(f32[3,16,640]{2,1,0:T(8,128)} %fields_ref.3) | copy-start | bytes 368644
  33.8 7.0 %copy-start.1 = (f32[3,16,640]{2,1,0:T(8,128)S(1)}, f32[3,16,640]{2,1,0:T(8,128)}, u32[]{:S(2)}) copy-start(f32[3,16,640]{2,1,0:T(8,128)} %kappa_ref.3) | copy-start | bytes 368644
  33.8 7.0 %copy-start.2 = (f32[3,2]{0,1:T(2,128)S(1)}, f32[3,2]{0,1:T(2,128)}, u32[]{:S(2)}) copy-start(f32[3,2]{0,1:T(2,128)} %param.11) | copy-start | bytes 76
  33.8 7.0 %copy-start.3 = (f32[3]{0:T(128)S(1)}, f32[3]{0:T(128)}, u32[]{:S(2)}) copy-start(f32[3]{0:T(128)} %precision_ref.1) | copy-start | bytes 40
  34.5 10.7 %all-to-all-start.2 = ((f32[8,32,128]{2,1,0:T(8,128)}), f32[8,32,128]{2,1,0:T(8,128)S(1)}, u32[]{:S(2)}, u32[]{:S(2)}) async-start(f32[8,32,128]{2,1,0:T(8,128)} %bitcast.6), calls=%async_computation.2 | async-start | bytes 262144 | tf_op jit(solution)/shard_map/all_to_all | solution.py:218

commit v6 on v5

--- a/solution.py
+++ b/solution.py
@@ -39,7 +39,7 @@
 
 
 def rounds(here, last):
-    return here < 2, (here == 0) | (here == last), here >= last - 1
+    return here < EARLY, (here < EARLY) | (here == last), here >= last - 1
 
 
 def likelihood_kernel(
@@ -187,7 +187,7 @@
     f32 = jnp.float32
     rows, columns = fields.shape[1:]
     spaces, groups = lax.axis_size("space"), lax.axis_size("years")
-    planes = [[z + (a + SUB // 2) % SUB for a in range(SUB)] for z in range(0, spaces, SUB)]
+    planes = [list(range(z, z + SUB)) for z in range(0, spaces, SUB)]
     cells = pl.pallas_call(
         cells_kernel,
         out_shape=jax.ShapeDtypeStruct((SUB, LANES), f32),
@@ -231,9 +231,10 @@
     inner_pairs = [(s, s ^ 1) for s in range(spaces)]
     outer_pairs = [(s, (s + (1 if s % 2 else -1)) % spaces) for s in range(spaces)]
     last = spaces - 1
-    early_pairs = [(0, 1), (1, 0), (last - 2, last - 1), (last - 1, last - 2)]
-    early_pairs += [pair for pair in outer_pairs if 2 < min(pair) and max(pair) < EARLY]
-    first_pairs = [pair for pair in inner_pairs if 1 < min(pair) and max(pair) < last - 1]
+    early_pairs = [pair for pair in inner_pairs if max(pair) < EARLY]
+    early_pairs += [(last - 2, last - 1), (last - 1, last - 2)]
+    first_pairs = [pair for pair in inner_pairs if EARLY <= min(pair) and max(pair) < last - 1]
+    first_pairs += [pair for pair in outer_pairs if 0 < min(pair) and max(pair) < EARLY]
     first_pairs += [(0, last), (last, 0)]
     second_pairs = [pair for pair in inner_pairs + outer_pairs if pair not in early_pairs + first_pairs]
     from_early = lax.ppermute(early, "space", early_pairs)

time: 46.4 us -> 46 us (level)
  the two profiles are of different devices: /device:TPU:8 before, /device:TPU:131 now
where the time goes in v6:
time: 46 us; the launch traced here: 45.5 us
  starting transfers between devices  35.2 us (77%)
  Pallas kernels  7.99 us (17%)
  waiting for transfers between devices  2.1 us (5%)
    all_to_all x2, starting transfers between devices, exchange(): lax.all_to_all(pieces, 'years', 0, 0, tiled=True, axis_index_groups=[order])  23.8 us
    all_to_all x1, starting transfers between devices, local(): lax.all_to_all(cells[:, None], 'space', 0, 0, tiled=True, axis_index_grou...  5.14 us
    ppermute x1, starting transfers between devices, local(): from_first = lax.ppermute(first, 'space', first_pairs)  2.88 us
    pallas_call x1, Pallas kernels, local(): pl.pallas_call(functools.partial(likelihood_kernel, end=spaces - 1), out_...  2.78 us
    pallas_call x1, Pallas kernels, local(): pl.pallas_call(functools.partial(prior_kernel, last=last), out_shape=jax....  2.38 us
    ppermute x1, starting transfers between devices, local(): lax.ppermute(lax.optimization_barrier(second), 'space', second_pairs)  2.08 us
    pallas_call x1, Pallas kernels, local(): pl.pallas_call(cells_kernel, out_shape=jax.ShapeDtypeStruct((SUB, LANES),...  1.41 us
    all_to_all x2, waiting for transfers between devices, exchange(): lax.all_to_all(pieces, 'years', 0, 0, tiled=True, axis_index_groups=[order])  1.39 us
  transfers between devices with their start and end apart: 7, of which 2 were waited for; matrix products, arithmetic and copies ran while one was open for 0% of the time, Pallas kernels for 13%

profile of v6, /device:TPU:131, one launch (start us, length us, event | category | flops | bytes accessed | tf_op | source)
XLA Modules:
  0.0 45.5 jit_solution(4282339032173873777)
XLA Ops:
  0.0 1.4 %cells.1 = f32[8,128]{1,0:T(8,128)} custom-call(s32[16,640]{1,0:T(8,128)} %mask_ref.3, s32[16,640]{1,0:T(8,128)} %counts_ref.3), custom_call_target="tpu_custom_call" | custom-call | flops 20480 | bytes 81920 | tf_op jit(solution)/shard_map/cells/pallas_call | solution.py:191
  1.4 5.1 %all-to-all-start.1 = ((f32[8,1,128]{2,1,0:T(1,128)}), f32[8,1,128]{2,1,0:T(1,128)S(1)}, u32[]{:S(2)}, u32[]{:S(2)}) async-start(f32[8,1,128]{2,1,0:T(1,128)} %bitcast.14), calls=%async_computation.1 | async-start | bytes 8192 | tf_op jit(solution)/shard_map/all_to_all | solution.py:199
  6.6 2.8 %likelihood.1 = (f32[256,128]{1,0:T(8,128)}, f32[6,8,640]{2,1,0:T(8,128)}, f32[6,8,640]{2,1,0:T(8,128)}, f32[6,8,640]{2,1,0:T(8,128)}) custom-call(s32[1]{0:T(128)} %bitcast.here_ref, s32[4]{0:T(128)} %valid_ref.1, f32[4,8,16,640]{3,2,1,0:T(8,128)} %maxima_ref.1, f32[3,16,640]{2,1,0:T(8,128)} %fields_ref.3, f32[3,16,640]{2,1,0:T(8,128)} %kappa_ref.3, ...), custom_call_target="tpu_custom_call" | custom-call | flops 99999997952 | bytes 1073741824 | tf_op jit(solution)/shard_map/likelihood/pallas_call | solution.py:206
  9.3 0.7 %all-to-all-done.1 = f32[8,1,128]{2,1,0:T(1,128)S(1)} async-done(((f32[8,1,128]{2,1,0:T(1,128)}), f32[8,1,128]{2,1,0:T(1,128)S(1)}, u32[]{:S(2)}, u32[]{:S(2)}) %all-to-all-start.1) | async-done | bytes 4128 | tf_op jit(solution)/shard_map/all_to_all | solution.py:199
  10.0 8.8 %all-to-all-start = ((f32[8,32,128]{2,1,0:T(8,128)}), f32[8,32,128]{2,1,0:T(8,128)S(1)}, u32[]{:S(2)}, u32[]{:S(2)}) async-start(f32[8,32,128]{2,1,0:T(8,128)} %bitcast.13), calls=%async_computation | async-start | bytes 262144 | tf_op jit(solution)/shard_map/all_to_all | solution.py:218
  18.9 0.7 %collective-permute-start.1 = (f32[6,8,640]{2,1,0:T(8,128)}, f32[6,8,640]{2,1,0:T(8,128)S(1)}, u32[]{:S(2)}, u32[]{:S(2)}) collective-permute-start(f32[6,8,640]{2,1,0:T(8,128)} %get-tuple-element.13), channel_id=1, source_target_pairs={{0,8},{8,0},{16,24},{24,16},{32,40},{40,32},{48,56},{56,48},{64,72... | collective-permute-start | bytes 368648 | tf_op jit(solution)/shard_map/ppermute | solution.py:240
  19.5 0.7 %collective-permute-start = (f32[8,128]{1,0:T(8,128)S(1)}, f32[8,128]{1,0:T(8,128)S(1)}, u32[]{:S(2)}, u32[]{:S(2)}) collective-permute-start(f32[8,128]{1,0:T(8,128)S(1)} %bitcast.15), channel_id=1, source_target_pairs={{0,0},{65,1},{130,2},{323,3},{260,4},{389,5},{454,6},{199,7},{8,8}... | collective-permute-start | bytes 12296 | tf_op jit(solution)/shard_map/ppermute | solution.py:230
  20.2 2.9 %collective-permute-start.2 = (f32[6,8,640]{2,1,0:T(8,128)}, f32[6,8,640]{2,1,0:T(8,128)S(1)}, u32[]{:S(2)}, u32[]{:S(2)}) collective-permute-start(f32[6,8,640]{2,1,0:T(8,128)} %get-tuple-element.17), channel_id=1, source_target_pairs={{128,136},{136,128},{144,152},{152,144},{160,168},{168,160},{176,1... | collective-permute-start | bytes 368648 | tf_op jit(solution)/shard_map/ppermute | solution.py:251
  23.1 2.1 %collective-permute-start.3 = (f32[6,8,640]{2,1,0:T(8,128)}, f32[6,8,640]{2,1,0:T(8,128)S(1)}, u32[]{:S(2)}, u32[]{:S(2)}) collective-permute-start(f32[6,8,640]{2,1,0:T(8,128)} %get-tuple-element.18), channel_id=1, source_target_pairs={{496,504},{504,496},{120,128},{128,120},{136,144},{144,136},{152,1... | collective-permute-start | bytes 368648 | tf_op jit(solution)/shard_map/ppermute | solution.py:252
  25.2 0.0 collective-permute-done.cells_ref
  25.2 0.0 collective-permute-done.1.early_ref
  25.2 0.0 all-to-all-done
  25.2 0.0 copy-start
  25.2 0.0 copy-start.1
  25.2 0.0 copy-start.2
  25.2 0.0 copy-start.3
  25.3 0.7 %middle.1 = f32[256,128]{1,0:T(8,128)} custom-call(f32[256,128]{1,0:T(8,128)S(1)} %bitcast.11, f32[8,128]{1,0:T(8,128)S(1)} %collective-permute-done.cells_ref), custom_call_target="tpu_custom_call" | custom-call | flops 99999997952 | bytes 1073741824 | tf_op jit(solution)/shard_map/middle/pallas_call | solution.py:242
  25.9 15.0 %all-to-all-start.2 = ((f32[8,32,128]{2,1,0:T(8,128)}), f32[8,32,128]{2,1,0:T(8,128)S(1)}, u32[]{:S(2)}, u32[]{:S(2)}) async-start(f32[8,32,128]{2,1,0:T(8,128)} %bitcast.6), calls=%async_computation.2 | async-start | bytes 262144 | tf_op jit(solution)/shard_map/all_to_all | solution.py:218
  40.9 0.0 collective-permute-done.2.first_ref
  40.9 0.0 collective-permute-done.3.second_ref
  40.9 0.0 copy-done
  40.9 2.4 %prior.1.refs_1_ = f32[3,16,640]{2,1,0:T(8,128)S(1)} custom-call(s32[1]{0:T(128)} %bitcast.here_ref, f32[2,3]{1,0:T(2,128)S(1)} %bitcast.12, f32[3]{0:T(128)S(1)} %copy-done.3, f32[3,16,640]{2,1,0:T(8,128)S(1)} %copy-done, f32[3,16,640]{2,1,0:T(8,128)S(1)} %copy-done.1, f32[6,8,640]{2,1,0:T(8,128)S(1)} %collective-permute-done.1.early_ref, ...), custom_call_target="tpu_custom_call" | custom-call | flops 99999997952 | bytes 1073741824 | tf_op jit(solution)/shard_map/prior/pallas_call | solution.py:255
  43.3 1.4 %all-to-all-done.2 = f32[8,32,128]{2,1,0:T(8,128)S(1)} async-done(((f32[8,32,128]{2,1,0:T(8,128)}), f32[8,32,128]{2,1,0:T(8,128)S(1)}, u32[]{:S(2)}, u32[]{:S(2)}) %all-to-all-start.2) | async-done | bytes 131104 | tf_op jit(solution)/shard_map/all_to_all | solution.py:218
  44.7 0.8 %final.1 = f32[3,16,640]{2,1,0:T(8,128)} custom-call(f32[256,128]{1,0:T(8,128)S(1)} %bitcast.10, f32[3,16,640]{2,1,0:T(8,128)S(1)} %prior.1.refs_1_), custom_call_target="tpu_custom_call" | custom-call | flops 61440 | bytes 368640 | tf_op jit(solution)/shard_map/final/pallas_call | solution.py:268
  (3 shorter events, 0.0 us)
Async XLA Ops:
  1.4 8.6 %all-to-all-start.1 = ((f32[8,1,128]{2,1,0:T(1,128)}), f32[8,1,128]{2,1,0:T(1,128)S(1)}, u32[]{:S(2)}, u32[]{:S(2)}) async-start(f32[8,1,128]{2,1,0:T(1,128)} %bitcast.14), calls=%async_computation.1 | async-start | bytes 8192 | tf_op jit(solution)/shard_map/all_to_all | solution.py:199
  10.0 15.2 %all-to-all-start = ((f32[8,32,128]{2,1,0:T(8,128)}), f32[8,32,128]{2,1,0:T(8,128)S(1)}, u32[]{:S(2)}, u32[]{:S(2)}) async-start(f32[8,32,128]{2,1,0:T(8,128)} %bitcast.13), calls=%async_computation | async-start | bytes 262144 | tf_op jit(solution)/shard_map/all_to_all | solution.py:218
  18.9 6.3 %collective-permute-start.1 = (f32[6,8,640]{2,1,0:T(8,128)}, f32[6,8,640]{2,1,0:T(8,128)S(1)}, u32[]{:S(2)}, u32[]{:S(2)}) collective-permute-start(f32[6,8,640]{2,1,0:T(8,128)} %get-tuple-element.13), channel_id=1, source_target_pairs={{0,8},{8,0},{16,24},{24,16},{32,40},{40,32},{48,56},{56,48},{64,72... | collective-permute-start | bytes 368648 | tf_op jit(solution)/shard_map/ppermute | solution.py:240
  19.5 5.6 %collective-permute-start = (f32[8,128]{1,0:T(8,128)S(1)}, f32[8,128]{1,0:T(8,128)S(1)}, u32[]{:S(2)}, u32[]{:S(2)}) collective-permute-start(f32[8,128]{1,0:T(8,128)S(1)} %bitcast.15), channel_id=1, source_target_pairs={{0,0},{65,1},{130,2},{323,3},{260,4},{389,5},{454,6},{199,7},{8,8}... | collective-permute-start | bytes 12296 | tf_op jit(solution)/shard_map/ppermute | solution.py:230
  20.2 20.7 %collective-permute-start.2 = (f32[6,8,640]{2,1,0:T(8,128)}, f32[6,8,640]{2,1,0:T(8,128)S(1)}, u32[]{:S(2)}, u32[]{:S(2)}) collective-permute-start(f32[6,8,640]{2,1,0:T(8,128)} %get-tuple-element.17), channel_id=1, source_target_pairs={{128,136},{136,128},{144,152},{152,144},{160,168},{168,160},{176,1... | collective-permute-start | bytes 368648 | tf_op jit(solution)/shard_map/ppermute | solution.py:251
  23.1 17.8 %collective-permute-start.3 = (f32[6,8,640]{2,1,0:T(8,128)}, f32[6,8,640]{2,1,0:T(8,128)S(1)}, u32[]{:S(2)}, u32[]{:S(2)}) collective-permute-start(f32[6,8,640]{2,1,0:T(8,128)} %get-tuple-element.18), channel_id=1, source_target_pairs={{496,504},{504,496},{120,128},{128,120},{136,144},{144,136},{152,1... | collective-permute-start | bytes 368648 | tf_op jit(solution)/shard_map/ppermute | solution.py:252
  25.2 15.7 %copy-start = (f32[3,16,640]{2,1,0:T(8,128)S(1)}, f32[3,16,640]{2,1,0:T(8,128)}, u32[]{:S(2)}) copy-start(f32[3,16,640]{2,1,0:T(8,128)} %fields_ref.3) | copy-start | bytes 368644
  25.2 15.7 %copy-start.1 = (f32[3,16,640]{2,1,0:T(8,128)S(1)}, f32[3,16,640]{2,1,0:T(8,128)}, u32[]{:S(2)}) copy-start(f32[3,16,640]{2,1,0:T(8,128)} %kappa_ref.3) | copy-start | bytes 368644
  25.2 15.7 %copy-start.2 = (f32[3,2]{0,1:T(2,128)S(1)}, f32[3,2]{0,1:T(2,128)}, u32[]{:S(2)}) copy-start(f32[3,2]{0,1:T(2,128)} %param.11) | copy-start | bytes 76
  25.2 15.7 %copy-start.3 = (f32[3]{0:T(128)S(1)}, f32[3]{0:T(128)}, u32[]{:S(2)}) copy-start(f32[3]{0:T(128)} %precision_ref.1) | copy-start | bytes 40
  25.9 18.8 %all-to-all-start.2 = ((f32[8,32,128]{2,1,0:T(8,128)}), f32[8,32,128]{2,1,0:T(8,128)S(1)}, u32[]{:S(2)}, u32[]{:S(2)}) async-start(f32[8,32,128]{2,1,0:T(8,128)} %bitcast.6), calls=%async_computation.2 | async-start | bytes 262144 | tf_op jit(solution)/shard_map/all_to_all | solution.py:218

commit v7 on v6

--- a/solution.py
+++ b/solution.py
@@ -13,7 +13,7 @@
 SUB = 8
 MIB = 1 << 20
 PIECE = 32
-EARLY = 16
+EARLY = 24
 PARTNER = (0, 1, 2, 5, 4, 6, 7, 3)
 CELL_ROW = 30
 YEAR_ROW = 31

time: 46 us -> 45.9 us (level)
  the two profiles are of different devices: /device:TPU:131 before, /device:TPU:16 now
where the time goes in v7:
time: 45.9 us; the launch traced here: 45.5 us
  starting transfers between devices  31.9 us (69%)
  Pallas kernels  7.99 us (17%)
  waiting for transfers between devices  5.41 us (12%)
    all_to_all x2, starting transfers between devices, exchange(): lax.all_to_all(pieces, 'years', 0, 0, tiled=True, axis_index_groups=[order])  15.7 us
    ppermute x1, starting transfers between devices, local(): from_first = lax.ppermute(first, 'space', first_pairs)  5.52 us
    all_to_all x1, starting transfers between devices, local(): lax.all_to_all(cells[:, None], 'space', 0, 0, tiled=True, axis_index_grou...  4.3 us
    ppermute x1, starting transfers between devices, local(): far_cells = lax.ppermute(plane_cells, ('space', 'years'), far)  3.77 us
    all_to_all x2, waiting for transfers between devices, exchange(): lax.all_to_all(pieces, 'years', 0, 0, tiled=True, axis_index_groups=[order])  2.92 us
    pallas_call x1, Pallas kernels, local(): pl.pallas_call(functools.partial(likelihood_kernel, end=spaces - 1), out_...  2.77 us
    all_to_all x1, waiting for transfers between devices, local(): lax.all_to_all(cells[:, None], 'space', 0, 0, tiled=True, axis_index_grou...  2.49 us
    pallas_call x1, Pallas kernels, local(): pl.pallas_call(functools.partial(prior_kernel, last=last), out_shape=jax....  2.38 us
  transfers between devices with their start and end apart: 7, of which 2 were waited for; matrix products, arithmetic and copies ran while one was open for 0% of the time, Pallas kernels for 13%

profile of v7, /device:TPU:16, one launch (start us, length us, event | category | flops | bytes accessed | tf_op | source)
XLA Modules:
  0.0 45.5 jit_solution(17273194888821541406)
XLA Ops:
  0.0 1.4 %cells.1 = f32[8,128]{1,0:T(8,128)} custom-call(s32[16,640]{1,0:T(8,128)} %mask_ref.3, s32[16,640]{1,0:T(8,128)} %counts_ref.3), custom_call_target="tpu_custom_call" | custom-call | flops 20480 | bytes 81920 | tf_op jit(solution)/shard_map/cells/pallas_call | solution.py:191
  1.4 4.3 %all-to-all-start.1 = ((f32[8,1,128]{2,1,0:T(1,128)}), f32[8,1,128]{2,1,0:T(1,128)S(1)}, u32[]{:S(2)}, u32[]{:S(2)}) async-start(f32[8,1,128]{2,1,0:T(1,128)} %bitcast.14), calls=%async_computation.1 | async-start | bytes 8192 | tf_op jit(solution)/shard_map/all_to_all | solution.py:199
  5.7 2.8 %likelihood.1 = (f32[256,128]{1,0:T(8,128)}, f32[6,8,640]{2,1,0:T(8,128)}, f32[6,8,640]{2,1,0:T(8,128)}, f32[6,8,640]{2,1,0:T(8,128)}) custom-call(s32[1]{0:T(128)} %bitcast.here_ref, s32[4]{0:T(128)} %valid_ref.1, f32[4,8,16,640]{3,2,1,0:T(8,128)} %maxima_ref.1, f32[3,16,640]{2,1,0:T(8,128)} %fields_ref.3, f32[3,16,640]{2,1,0:T(8,128)} %kappa_ref.3, ...), custom_call_target="tpu_custom_call" | custom-call | flops 99999997952 | bytes 1073741824 | tf_op jit(solution)/shard_map/likelihood/pallas_call | solution.py:206
  8.5 2.5 %all-to-all-done.1 = f32[8,1,128]{2,1,0:T(1,128)S(1)} async-done(((f32[8,1,128]{2,1,0:T(1,128)}), f32[8,1,128]{2,1,0:T(1,128)S(1)}, u32[]{:S(2)}, u32[]{:S(2)}) %all-to-all-start.1) | async-done | bytes 4128 | tf_op jit(solution)/shard_map/all_to_all | solution.py:199
  11.0 9.4 %all-to-all-start = ((f32[8,32,128]{2,1,0:T(8,128)}), f32[8,32,128]{2,1,0:T(8,128)S(1)}, u32[]{:S(2)}, u32[]{:S(2)}) async-start(f32[8,32,128]{2,1,0:T(8,128)} %bitcast.13), calls=%async_computation | async-start | bytes 262144 | tf_op jit(solution)/shard_map/all_to_all | solution.py:218
  20.4 1.9 %collective-permute-start.1 = (f32[6,8,640]{2,1,0:T(8,128)}, f32[6,8,640]{2,1,0:T(8,128)S(1)}, u32[]{:S(2)}, u32[]{:S(2)}) collective-permute-start(f32[6,8,640]{2,1,0:T(8,128)} %get-tuple-element.13), channel_id=1, source_target_pairs={{0,8},{8,0},{16,24},{24,16},{32,40},{40,32},{48,56},{56,48},{64,72... | collective-permute-start | bytes 368648 | tf_op jit(solution)/shard_map/ppermute | solution.py:240
  22.3 3.8 %collective-permute-start = (f32[8,128]{1,0:T(8,128)S(1)}, f32[8,128]{1,0:T(8,128)S(1)}, u32[]{:S(2)}, u32[]{:S(2)}) collective-permute-start(f32[8,128]{1,0:T(8,128)S(1)} %bitcast.15), channel_id=1, source_target_pairs={{0,0},{65,1},{130,2},{323,3},{260,4},{389,5},{454,6},{199,7},{8,8}... | collective-permute-start | bytes 12296 | tf_op jit(solution)/shard_map/ppermute | solution.py:230
  26.1 5.5 %collective-permute-start.2 = (f32[6,8,640]{2,1,0:T(8,128)}, f32[6,8,640]{2,1,0:T(8,128)S(1)}, u32[]{:S(2)}, u32[]{:S(2)}) collective-permute-start(f32[6,8,640]{2,1,0:T(8,128)} %get-tuple-element.17), channel_id=1, source_target_pairs={{192,200},{200,192},{208,216},{216,208},{224,232},{232,224},{240,2... | collective-permute-start | bytes 368648 | tf_op jit(solution)/shard_map/ppermute | solution.py:251
  31.6 0.7 %collective-permute-start.3 = (f32[6,8,640]{2,1,0:T(8,128)}, f32[6,8,640]{2,1,0:T(8,128)S(1)}, u32[]{:S(2)}, u32[]{:S(2)}) collective-permute-start(f32[6,8,640]{2,1,0:T(8,128)} %get-tuple-element.18), channel_id=1, source_target_pairs={{496,504},{504,496},{184,192},{192,184},{200,208},{208,200},{216,2... | collective-permute-start | bytes 368648 | tf_op jit(solution)/shard_map/ppermute | solution.py:252
  32.3 0.0 collective-permute-done.cells_ref
  32.3 0.0 collective-permute-done.1.early_ref
  32.3 0.0 all-to-all-done
  32.3 0.0 copy-start
  32.3 0.0 copy-start.1
  32.3 0.0 copy-start.2
  32.4 0.0 copy-start.3
  32.4 0.7 %middle.1 = f32[256,128]{1,0:T(8,128)} custom-call(f32[256,128]{1,0:T(8,128)S(1)} %bitcast.11, f32[8,128]{1,0:T(8,128)S(1)} %collective-permute-done.cells_ref), custom_call_target="tpu_custom_call" | custom-call | flops 99999997952 | bytes 1073741824 | tf_op jit(solution)/shard_map/middle/pallas_call | solution.py:242
  33.0 6.3 %all-to-all-start.2 = ((f32[8,32,128]{2,1,0:T(8,128)}), f32[8,32,128]{2,1,0:T(8,128)S(1)}, u32[]{:S(2)}, u32[]{:S(2)}) async-start(f32[8,32,128]{2,1,0:T(8,128)} %bitcast.6), calls=%async_computation.2 | async-start | bytes 262144 | tf_op jit(solution)/shard_map/all_to_all | solution.py:218
  39.4 0.0 collective-permute-done.2.first_ref
  39.4 0.0 collective-permute-done.3.second_ref
  39.4 0.0 copy-done
  39.4 2.4 %prior.1.refs_1_ = f32[3,16,640]{2,1,0:T(8,128)S(1)} custom-call(s32[1]{0:T(128)} %bitcast.here_ref, f32[2,3]{1,0:T(2,128)S(1)} %bitcast.12, f32[3]{0:T(128)S(1)} %copy-done.3, f32[3,16,640]{2,1,0:T(8,128)S(1)} %copy-done, f32[3,16,640]{2,1,0:T(8,128)S(1)} %copy-done.1, f32[6,8,640]{2,1,0:T(8,128)S(1)} %collective-permute-done.1.early_ref, ...), custom_call_target="tpu_custom_call" | custom-call | flops 99999997952 | bytes 1073741824 | tf_op jit(solution)/shard_map/prior/pallas_call | solution.py:255
  41.8 2.9 %all-to-all-done.2 = f32[8,32,128]{2,1,0:T(8,128)S(1)} async-done(((f32[8,32,128]{2,1,0:T(8,128)}), f32[8,32,128]{2,1,0:T(8,128)S(1)}, u32[]{:S(2)}, u32[]{:S(2)}) %all-to-all-start.2) | async-done | bytes 131104 | tf_op jit(solution)/shard_map/all_to_all | solution.py:218
  44.7 0.8 %final.1 = f32[3,16,640]{2,1,0:T(8,128)} custom-call(f32[256,128]{1,0:T(8,128)S(1)} %bitcast.10, f32[3,16,640]{2,1,0:T(8,128)S(1)} %prior.1.refs_1_), custom_call_target="tpu_custom_call" | custom-call | flops 61440 | bytes 368640 | tf_op jit(solution)/shard_map/final/pallas_call | solution.py:268
  (3 shorter events, 0.0 us)
Async XLA Ops:
  1.4 9.6 %all-to-all-start.1 = ((f32[8,1,128]{2,1,0:T(1,128)}), f32[8,1,128]{2,1,0:T(1,128)S(1)}, u32[]{:S(2)}, u32[]{:S(2)}) async-start(f32[8,1,128]{2,1,0:T(1,128)} %bitcast.14), calls=%async_computation.1 | async-start | bytes 8192 | tf_op jit(solution)/shard_map/all_to_all | solution.py:199
  11.0 21.3 %all-to-all-start = ((f32[8,32,128]{2,1,0:T(8,128)}), f32[8,32,128]{2,1,0:T(8,128)S(1)}, u32[]{:S(2)}, u32[]{:S(2)}) async-start(f32[8,32,128]{2,1,0:T(8,128)} %bitcast.13), calls=%async_computation | async-start | bytes 262144 | tf_op jit(solution)/shard_map/all_to_all | solution.py:218
  20.4 11.9 %collective-permute-start.1 = (f32[6,8,640]{2,1,0:T(8,128)}, f32[6,8,640]{2,1,0:T(8,128)S(1)}, u32[]{:S(2)}, u32[]{:S(2)}) collective-permute-start(f32[6,8,640]{2,1,0:T(8,128)} %get-tuple-element.13), channel_id=1, source_target_pairs={{0,8},{8,0},{16,24},{24,16},{32,40},{40,32},{48,56},{56,48},{64,72... | collective-permute-start | bytes 368648 | tf_op jit(solution)/shard_map/ppermute | solution.py:240
  22.3 10.0 %collective-permute-start = (f32[8,128]{1,0:T(8,128)S(1)}, f32[8,128]{1,0:T(8,128)S(1)}, u32[]{:S(2)}, u32[]{:S(2)}) collective-permute-start(f32[8,128]{1,0:T(8,128)S(1)} %bitcast.15), channel_id=1, source_target_pairs={{0,0},{65,1},{130,2},{323,3},{260,4},{389,5},{454,6},{199,7},{8,8}... | collective-permute-start | bytes 12296 | tf_op jit(solution)/shard_map/ppermute | solution.py:230
  26.1 13.3 %collective-permute-start.2 = (f32[6,8,640]{2,1,0:T(8,128)}, f32[6,8,640]{2,1,0:T(8,128)S(1)}, u32[]{:S(2)}, u32[]{:S(2)}) collective-permute-start(f32[6,8,640]{2,1,0:T(8,128)} %get-tuple-element.17), channel_id=1, source_target_pairs={{192,200},{200,192},{208,216},{216,208},{224,232},{232,224},{240,2... | collective-permute-start | bytes 368648 | tf_op jit(solution)/shard_map/ppermute | solution.py:251
  31.6 7.7 %collective-permute-start.3 = (f32[6,8,640]{2,1,0:T(8,128)}, f32[6,8,640]{2,1,0:T(8,128)S(1)}, u32[]{:S(2)}, u32[]{:S(2)}) collective-permute-start(f32[6,8,640]{2,1,0:T(8,128)} %get-tuple-element.18), channel_id=1, source_target_pairs={{496,504},{504,496},{184,192},{192,184},{200,208},{208,200},{216,2... | collective-permute-start | bytes 368648 | tf_op jit(solution)/shard_map/ppermute | solution.py:252
  32.3 7.0 %copy-start = (f32[3,16,640]{2,1,0:T(8,128)S(1)}, f32[3,16,640]{2,1,0:T(8,128)}, u32[]{:S(2)}) copy-start(f32[3,16,640]{2,1,0:T(8,128)} %fields_ref.3) | copy-start | bytes 368644
  32.3 7.0 %copy-start.1 = (f32[3,16,640]{2,1,0:T(8,128)S(1)}, f32[3,16,640]{2,1,0:T(8,128)}, u32[]{:S(2)}) copy-start(f32[3,16,640]{2,1,0:T(8,128)} %kappa_ref.3) | copy-start | bytes 368644
  32.3 7.0 %copy-start.2 = (f32[3,2]{0,1:T(2,128)S(1)}, f32[3,2]{0,1:T(2,128)}, u32[]{:S(2)}) copy-start(f32[3,2]{0,1:T(2,128)} %param.11) | copy-start | bytes 76
  32.4 7.0 %copy-start.3 = (f32[3]{0:T(128)S(1)}, f32[3]{0:T(128)}, u32[]{:S(2)}) copy-start(f32[3]{0:T(128)} %precision_ref.1) | copy-start | bytes 40
  33.0 11.7 %all-to-all-start.2 = ((f32[8,32,128]{2,1,0:T(8,128)}), f32[8,32,128]{2,1,0:T(8,128)S(1)}, u32[]{:S(2)}, u32[]{:S(2)}) async-start(f32[8,32,128]{2,1,0:T(8,128)} %bitcast.6), calls=%async_computation.2 | async-start | bytes 262144 | tf_op jit(solution)/shard_map/all_to_all | solution.py:218
